TPU v7x, 256 devices: a whole 4x4x8 slice. The times are simulated.
256 devices in a mesh: row: 16 (over x_lo, y, core), col: 16 (over x_hi, z).
Axes of the slice: x: 4 (x_hi: 2, x_lo: 2; x = x_hi * 2 + x_lo), y: 4, z: 8, core: 2. Of those that a mesh axis runs over, the one named last changes fastest.
Arguments:
- object_slices: float32 [2, 2, 2048, 2048], P(None, None, 'row', 'col'), may hold values from -4 to 4
- probe: float32 [2, 128, 128], replicated, may hold values from -5 to 5
- phase: float32 [128, 128], replicated, may hold values from -3.140625 to 3.140625
- positions: int32 [16, 16, 4, 2], P('row', 'col'), may hold values from 0 to 127
- counts: int32 [16, 16], P('row', 'col'), may hold values from 1 to 4
- measured: float32 [16, 16, 4, 128, 128], P('row', 'col'), may hold values from 0.2 to 4
Outputs:
- updated: float32 [2, 2, 2048, 2048], P(None, None, 'row', 'col')
Inputs may be any that keep to these rules, and one draw needn't show every extreme that they name: Slots k with k >= counts of the tile are padding and do not contribute. `positions`: a window may reach up to 127 pixels into the tiles below, to the right and diagonally below right.
All inputs are finite; a program needn't handle non-finite values.
Results may differ from a plain program's by a relative error of at most 0.0003.
Values sent between devices are 32-bit elements; how exact they have to be, the bound alone decides.
A program may use at most 64 MiB of HBM per device.

v0:
```python
import jax
import jax.numpy as jnp
from jax import lax
from jax.sharding import PartitionSpec as P

ITERS = 2


step_rate = 0.02


def passed_along(value, axis, steps):
    count = lax.axis_size(axis)
    pairs = [(source, (source + steps) % count) for source in range(count)]
    return lax.ppermute(value, axis, pairs)


def dft_tables(width):
    index = jnp.arange(width, dtype=jnp.int32)
    product = index[:, None] * index[None, :] % width
    angle = product.astype(jnp.float32) * (-2.0 * jnp.pi / width)
    scale = 1.0 / jnp.sqrt(jnp.float32(width))
    return (jnp.cos(angle) * scale, jnp.sin(angle) * scale)


def transform(real, imag, table_re, table_im):
    high = lax.Precision.HIGHEST
    left_re = jnp.einsum("ij,njk->nik", table_re, real, precision=high) - jnp.einsum(
        "ij,njk->nik", table_im, imag, precision=high
    )
    left_im = jnp.einsum("ij,njk->nik", table_re, imag, precision=high) + jnp.einsum(
        "ij,njk->nik", table_im, real, precision=high
    )
    out_re = jnp.einsum("nij,jk->nik", left_re, table_re, precision=high) - jnp.einsum(
        "nij,jk->nik", left_im, table_im, precision=high
    )
    out_im = jnp.einsum("nij,jk->nik", left_re, table_im, precision=high) + jnp.einsum(
        "nij,jk->nik", left_im, table_re, precision=high
    )
    return (out_re, out_im)


def local_loss(extended, positions, live, probe, phase, measured):
    width = probe.shape[-1]
    layers = extended.shape[0]
    table_re, table_im = dft_tables(width)

    def window(corner):
        zero = jnp.zeros((), jnp.int32)
        return lax.dynamic_slice(
            extended, (zero, zero, corner[0], corner[1]), (layers, 2, width, width)
        )

    windows = jax.vmap(window)(positions)
    wave_re = jnp.broadcast_to(probe[0], windows[:, 0, 0].shape)
    wave_im = jnp.broadcast_to(probe[1], windows[:, 0, 0].shape)
    prop_re = jnp.cos(phase)
    prop_im = jnp.sin(phase)
    for layer in range(layers):
        obj_re = windows[:, layer, 0]
        obj_im = windows[:, layer, 1]
        wave_re, wave_im = (
            wave_re * obj_re - wave_im * obj_im,
            wave_re * obj_im + wave_im * obj_re,
        )
        if layer + 1 < layers:
            spec_re, spec_im = transform(wave_re, wave_im, table_re, table_im)
            spec_re, spec_im = (
                spec_re * prop_re - spec_im * prop_im,
                spec_re * prop_im + spec_im * prop_re,
            )
            wave_re, wave_im = transform(spec_re, spec_im, table_re, -table_im)
    far_re, far_im = transform(wave_re, wave_im, table_re, table_im)
    misfit = far_re * far_re + far_im * far_im - measured
    return 0.5 * jnp.sum(live[:, None, None] * misfit * misfit)


def fetch_strips(current):
    right = passed_along(current, "col", -1)
    wide = jnp.concatenate([current, right], axis=-1)
    below = passed_along(wide, "row", -1)
    return jnp.concatenate([wide, below], axis=-2)


def per_device(object_slices, probe, phase, positions, counts, measured):
    tile = object_slices.shape[-1]
    width = probe.shape[-1]
    corners = positions[0, 0]
    slots = corners.shape[0]
    live = (jnp.arange(slots, dtype=jnp.int32) < counts[0, 0]).astype(jnp.float32)
    intensity = measured[0, 0]

    def gradient_of(extended):
        loss, pull = jax.vjp(
            lambda e: local_loss(e, corners, live, probe, phase, intensity), extended
        )
        return pull(jnp.ones_like(loss))[0]

    current = object_slices
    for step in range(ITERS):
        extended = fetch_strips(current)
        gradient_list = gradient_of(extended)
        bottom = passed_along(gradient_list[..., tile:, :], "row", 1)
        upper = gradient_list[..., :tile, :].at[..., :width, :].add(bottom)
        side = passed_along(upper[..., tile:], "col", 1)
        owned = upper[..., :tile].at[..., :width].add(side)
        current = current - step_rate * owned
    return current


def solution(mesh):
    return jax.shard_map(
        per_device,
        mesh=mesh,
        in_specs=(
            P(None, None, "row", "col"),
            P(),
            P(),
            P("row", "col", None, None),
            P("row", "col"),
            P("row", "col", None, None, None),
        ),
        out_specs=P(None, None, "row", "col"),
        check_vma=False,
    )
```

profile of v0, /device:TPU:2, one launch (start us, length us, event | category | flops | bytes accessed | tf_op | source)
XLA Modules:
  0.0 253.2 jit_solution(16779819763989072652)
XLA Ops:
  0.0 7.4 %collective-permute-start = (f32[2,2,128,128]{3,2,1,0:T(8,128)}, f32[2,2,128,128]{3,2,1,0:T(8,128)S(1)}, u32[]{:S(2)}, u32[]{:S(2)}) collective-permute-start(f32[2,2,128,128]{3,2,1,0:T(8,128)} %param.22), channel_id=1, source_target_pairs={{0,15},{1,0},{2,1},{3,2},{4,3},{5,4},{6,5},{7,6},{8,7},{9,8},{10,9... | collective-permute-start | bytes 786440 | tf_op jit(solution)/shard_map/ppermute | solution.py:15
  16.9 5.6 %collective-permute-done.1 = f32[2,2,128,256]{3,2,1,0:T(8,128)S(1)} collective-permute-done((f32[2,2,128,256]{3,2,1,0:T(8,128)S(1)}, f32[2,2,128,256]{3,2,1,0:T(8,128)S(1)}, u32[]{:S(2)}, u32[]{:S(2)}) %collective-permute-start.1) | collective-permute-done | bytes 524320 | tf_op jit(solution)/shard_map/ppermute | solution.py:15
  22.7 8.1 %while.12 = (s32[]{:T(128)}, f32[2,2,256,256]{3,2,1,0:T(8,128)S(1)}, s32[4,4]{1,0:T(4,128)S(1)}, f32[4,2,2,128,128]{4,3,0,2,1:T(8,128)S(1)}, s32[]{:T(128)}) while((s32[]{:T(128)}, f32[2,2,256,256]{3,2,1,0:T(8,128)S(1)}, s32[4,4]{1,0:T(4,128)S(1)}, f32[4,2,2,128,128]{4,3,0,2,1:T(8,128)S(1)}, s32[]{:T(128)}) %tuple.115), condition=%wide.while_cond.4, body=%wide.while_body.4.sunk | while | flops 2 | bytes 524413 | solution.py:50
  65.9 42.0 %while.14 = (s32[]{:T(128)}, f32[2,2,256,256]{3,2,1,0:T(8,128)S(1)}, s32[4,4]{1,0:T(4,128)S(1)}, f32[4,2,2,128,128]{4,3,0,2,1:T(8,128)S(1)}, s32[]{:T(128)}, /*index=5*/s32[4]{0:T(128)S(1)}, s32[]{:T(128)}) while((s32[]{:T(128)}, f32[2,2,256,256]{3,2,1,0:T(8,128)S(1)}, s32[4,4]{1,0:T(4,128)S(1)}, f32[4,2,2,128,128]{4,3,0,2,1:T(8,128)S(1)}, ...), condition=%wide.while_cond.6, body=%wide.while_body.6.sunk | while | flops 131101 | bytes 1310915 | solution.py:50
  66.6 3.2 %and_reduce_fusion.4 = pred[]{:T(512)} fusion(s32[4]{0:T(128)S(1)} %get-tuple-element.361, s32[1]{0:T(128)} %bitcast.547, s32[1]{0:T(128)} %bitcast.548, s32[1]{0:T(128)} %bitcast.549, s32[1]{0:T(128)} %bitcast.550), kind=kLoop, calls=%fused_computation.5.clone.1 | loop fusion | flops 27 | bytes 33 | tf_op jit(solution)/shard_map/transpose(jvp(vmap()))/scatter-add
  71.9 4.5 %dynamic-update-slice.28 = f32[2,2,256,256]{3,2,1,0:T(8,128)S(1)} dynamic-update-slice(f32[2,2,256,256]{3,2,1,0:T(8,128)S(1)} %get-tuple-element.350, f32[2,2,128,128]{3,2,1,0:T(8,128)S(1)} %add_select_fusion.5, s32[]{:T(128)} %constant.156.clone.1..sunk, s32[]{:T(128)} %constant.156.clone.1..sunk, s32[]{:T(128)} %bitcast.545, s32[]{:T(128)} %bitcast.546) | dynamic-update-slice | bytes 524292 | tf_op jit(solution)/shard_map/transpose(jvp(vmap()))/scatter-add
  82.4 4.5 %dynamic-update-slice.28 = f32[2,2,256,256]{3,2,1,0:T(8,128)S(1)} dynamic-update-slice(f32[2,2,256,256]{3,2,1,0:T(8,128)S(1)} %get-tuple-element.350, f32[2,2,128,128]{3,2,1,0:T(8,128)S(1)} %add_select_fusion.5, s32[]{:T(128)} %constant.156.clone.1..sunk, s32[]{:T(128)} %constant.156.clone.1..sunk, s32[]{:T(128)} %bitcast.545, s32[]{:T(128)} %bitcast.546) | dynamic-update-slice | bytes 524292 | tf_op jit(solution)/shard_map/transpose(jvp(vmap()))/scatter-add
  87.6 3.2 %and_reduce_fusion.4 = pred[]{:T(512)} fusion(s32[4]{0:T(128)S(1)} %get-tuple-element.361, s32[1]{0:T(128)} %bitcast.547, s32[1]{0:T(128)} %bitcast.548, s32[1]{0:T(128)} %bitcast.549, s32[1]{0:T(128)} %bitcast.550), kind=kLoop, calls=%fused_computation.5.clone.1 | loop fusion | flops 27 | bytes 33 | tf_op jit(solution)/shard_map/transpose(jvp(vmap()))/scatter-add
  92.9 4.4 %dynamic-update-slice.28 = f32[2,2,256,256]{3,2,1,0:T(8,128)S(1)} dynamic-update-slice(f32[2,2,256,256]{3,2,1,0:T(8,128)S(1)} %get-tuple-element.350, f32[2,2,128,128]{3,2,1,0:T(8,128)S(1)} %add_select_fusion.5, s32[]{:T(128)} %constant.156.clone.1..sunk, s32[]{:T(128)} %constant.156.clone.1..sunk, s32[]{:T(128)} %bitcast.545, s32[]{:T(128)} %bitcast.546) | dynamic-update-slice | bytes 524292 | tf_op jit(solution)/shard_map/transpose(jvp(vmap()))/scatter-add
  98.0 3.2 %and_reduce_fusion.4 = pred[]{:T(512)} fusion(s32[4]{0:T(128)S(1)} %get-tuple-element.361, s32[1]{0:T(128)} %bitcast.547, s32[1]{0:T(128)} %bitcast.548, s32[1]{0:T(128)} %bitcast.549, s32[1]{0:T(128)} %bitcast.550), kind=kLoop, calls=%fused_computation.5.clone.1 | loop fusion | flops 27 | bytes 33 | tf_op jit(solution)/shard_map/transpose(jvp(vmap()))/scatter-add
  103.3 4.6 %dynamic-update-slice.28 = f32[2,2,256,256]{3,2,1,0:T(8,128)S(1)} dynamic-update-slice(f32[2,2,256,256]{3,2,1,0:T(8,128)S(1)} %get-tuple-element.350, f32[2,2,128,128]{3,2,1,0:T(8,128)S(1)} %add_select_fusion.5, s32[]{:T(128)} %constant.156.clone.1..sunk, s32[]{:T(128)} %constant.156.clone.1..sunk, s32[]{:T(128)} %bitcast.545, s32[]{:T(128)} %bitcast.546) | dynamic-update-slice | bytes 524292 | tf_op jit(solution)/shard_map/transpose(jvp(vmap()))/scatter-add
  108.0 10.8 %collective-permute-done.2 = f32[2,2,128,256]{3,2,1,0:T(8,128)S(1)} collective-permute-done((f32[2,2,128,256]{3,2,1,0:T(8,128)S(1)}, f32[2,2,128,256]{3,2,1,0:T(8,128)S(1)}, u32[]{:S(2)}, u32[]{:S(2)}) %collective-permute-start.2) | collective-permute-done | bytes 524320 | tf_op jit(solution)/shard_map/ppermute | solution.py:15
  119.1 10.2 %collective-permute-done.3 = f32[2,2,128,128]{3,2,1,0:T(8,128)S(1)} collective-permute-done((f32[2,2,128,128]{3,2,1,0:T(8,128)S(1)}, f32[2,2,128,128]{3,2,1,0:T(8,128)S(1)}, u32[]{:S(2)}, u32[]{:S(2)}) %collective-permute-start.3) | collective-permute-done | bytes 262176 | tf_op jit(solution)/shard_map/ppermute | solution.py:15
  131.8 4.4 %collective-permute-done.4 = f32[2,2,128,128]{3,2,1,0:T(8,128)S(1)} collective-permute-done((f32[2,2,128,128]{3,2,1,0:T(8,128)S(1)}, f32[2,2,128,128]{3,2,1,0:T(8,128)S(1)}, u32[]{:S(2)}, u32[]{:S(2)}) %collective-permute-start.4) | collective-permute-done | bytes 262176 | tf_op jit(solution)/shard_map/ppermute | solution.py:15
  139.0 6.7 %collective-permute-done.5 = f32[2,2,128,256]{3,2,1,0:T(8,128)S(1)} collective-permute-done((f32[2,2,128,256]{3,2,1,0:T(8,128)S(1)}, f32[2,2,128,256]{3,2,1,0:T(8,128)S(1)}, u32[]{:S(2)}, u32[]{:S(2)}) %collective-permute-start.5) | collective-permute-done | bytes 524320 | tf_op jit(solution)/shard_map/ppermute | solution.py:15
  145.8 8.6 %while.13 = (s32[]{:T(128)}, f32[2,2,256,256]{3,2,1,0:T(8,128)S(1)}, s32[4,4]{1,0:T(4,128)S(1)}, f32[4,2,2,128,128]{4,3,0,2,1:T(8,128)S(1)}, s32[]{:T(128)}) while((s32[]{:T(128)}, f32[2,2,256,256]{3,2,1,0:T(8,128)S(1)}, s32[4,4]{1,0:T(4,128)S(1)}, f32[4,2,2,128,128]{4,3,0,2,1:T(8,128)S(1)}, s32[]{:T(128)}) %tuple.130), condition=%wide.while_cond.5, body=%wide.while_body.5.sunk | while | flops 2 | bytes 524413 | solution.py:50
  189.1 42.0 %while.15 = (s32[]{:T(128)}, f32[2,2,256,256]{3,2,1,0:T(8,128)S(1)}, s32[4,4]{1,0:T(4,128)S(1)}, f32[4,2,2,128,128]{4,3,0,2,1:T(8,128)S(1)}, s32[]{:T(128)}, /*index=5*/s32[4]{0:T(128)S(1)}, s32[]{:T(128)}) while((s32[]{:T(128)}, f32[2,2,256,256]{3,2,1,0:T(8,128)S(1)}, s32[4,4]{1,0:T(4,128)S(1)}, f32[4,2,2,128,128]{4,3,0,2,1:T(8,128)S(1)}, ...), condition=%wide.while_cond.7, body=%wide.while_body.7.sunk | while | flops 131101 | bytes 1310915 | solution.py:50
  195.0 4.5 %dynamic-update-slice.29 = f32[2,2,256,256]{3,2,1,0:T(8,128)S(1)} dynamic-update-slice(f32[2,2,256,256]{3,2,1,0:T(8,128)S(1)} %get-tuple-element.386, f32[2,2,128,128]{3,2,1,0:T(8,128)S(1)} %add_select_fusion.6, s32[]{:T(128)} %constant.156.clone.1..sunk.1, s32[]{:T(128)} %constant.156.clone.1..sunk.1, s32[]{:T(128)} %bitcast.552, s32[]{:T(128)} %bitcast.553) | dynamic-update-slice | bytes 524292 | tf_op jit(solution)/shard_map/transpose(jvp(vmap()))/scatter-add
  200.3 3.2 %and_reduce_fusion.5 = pred[]{:T(512)} fusion(s32[4]{0:T(128)S(1)} %get-tuple-element.397, s32[1]{0:T(128)} %bitcast.554, s32[1]{0:T(128)} %bitcast.555, s32[1]{0:T(128)} %bitcast.556, s32[1]{0:T(128)} %bitcast.557), kind=kLoop, calls=%fused_computation.8.clone.1 | loop fusion | flops 27 | bytes 33 | tf_op jit(solution)/shard_map/transpose(jvp(vmap()))/scatter-add
  205.6 4.5 %dynamic-update-slice.29 = f32[2,2,256,256]{3,2,1,0:T(8,128)S(1)} dynamic-update-slice(f32[2,2,256,256]{3,2,1,0:T(8,128)S(1)} %get-tuple-element.386, f32[2,2,128,128]{3,2,1,0:T(8,128)S(1)} %add_select_fusion.6, s32[]{:T(128)} %constant.156.clone.1..sunk.1, s32[]{:T(128)} %constant.156.clone.1..sunk.1, s32[]{:T(128)} %bitcast.552, s32[]{:T(128)} %bitcast.553) | dynamic-update-slice | bytes 524292 | tf_op jit(solution)/shard_map/transpose(jvp(vmap()))/scatter-add
  216.1 4.4 %dynamic-update-slice.29 = f32[2,2,256,256]{3,2,1,0:T(8,128)S(1)} dynamic-update-slice(f32[2,2,256,256]{3,2,1,0:T(8,128)S(1)} %get-tuple-element.386, f32[2,2,128,128]{3,2,1,0:T(8,128)S(1)} %add_select_fusion.6, s32[]{:T(128)} %constant.156.clone.1..sunk.1, s32[]{:T(128)} %constant.156.clone.1..sunk.1, s32[]{:T(128)} %bitcast.552, s32[]{:T(128)} %bitcast.553) | dynamic-update-slice | bytes 524292 | tf_op jit(solution)/shard_map/transpose(jvp(vmap()))/scatter-add
  226.5 4.6 %dynamic-update-slice.29 = f32[2,2,256,256]{3,2,1,0:T(8,128)S(1)} dynamic-update-slice(f32[2,2,256,256]{3,2,1,0:T(8,128)S(1)} %get-tuple-element.386, f32[2,2,128,128]{3,2,1,0:T(8,128)S(1)} %add_select_fusion.6, s32[]{:T(128)} %constant.156.clone.1..sunk.1, s32[]{:T(128)} %constant.156.clone.1..sunk.1, s32[]{:T(128)} %bitcast.552, s32[]{:T(128)} %bitcast.553) | dynamic-update-slice | bytes 524292 | tf_op jit(solution)/shard_map/transpose(jvp(vmap()))/scatter-add
  231.2 10.8 %collective-permute-done.6 = f32[2,2,128,256]{3,2,1,0:T(8,128)S(1)} collective-permute-done((f32[2,2,128,256]{3,2,1,0:T(8,128)S(1)}, f32[2,2,128,256]{3,2,1,0:T(8,128)S(1)}, u32[]{:S(2)}, u32[]{:S(2)}) %collective-permute-start.6) | collective-permute-done | bytes 524320 | tf_op jit(solution)/shard_map/ppermute | solution.py:15
  242.3 10.0 %collective-permute-done.7 = f32[2,2,128,128]{3,2,1,0:T(8,128)S(1)} collective-permute-done((f32[2,2,128,128]{3,2,1,0:T(8,128)S(1)}, f32[2,2,128,128]{3,2,1,0:T(8,128)S(1)}, u32[]{:S(2)}, u32[]{:S(2)}) %collective-permute-start.7) | collective-permute-done | bytes 262176 | tf_op jit(solution)/shard_map/ppermute | solution.py:15
  (201 shorter events, 135.7 us)
Async XLA Ops:
  0.0 13.3 %collective-permute-start = (f32[2,2,128,128]{3,2,1,0:T(8,128)}, f32[2,2,128,128]{3,2,1,0:T(8,128)S(1)}, u32[]{:S(2)}, u32[]{:S(2)}) collective-permute-start(f32[2,2,128,128]{3,2,1,0:T(8,128)} %param.22), channel_id=1, source_target_pairs={{0,15},{1,0},{2,1},{3,2},{4,3},{5,4},{6,5},{7,6},{8,7},{9,8},{10,9... | collective-permute-start | bytes 786440 | tf_op jit(solution)/shard_map/ppermute | solution.py:15
  8.4 0.7 copy-start.6
  10.0 0.7 copy-start.7
  10.7 5.2 %copy-start.2 = (f32[2,128,128]{2,1,0:T(8,128)S(1)}, f32[2,128,128]{2,1,0:T(8,128)}, u32[]{:S(2)}) copy-start(f32[2,128,128]{2,1,0:T(8,128)} %param.23) | copy-start | bytes 393220
  13.3 9.2 %collective-permute-start.1 = (f32[2,2,128,256]{3,2,1,0:T(8,128)S(1)}, f32[2,2,128,256]{3,2,1,0:T(8,128)S(1)}, u32[]{:S(2)}, u32[]{:S(2)}) collective-permute-start(f32[2,2,128,256]{3,2,1,0:T(8,128)S(1)} %constant_dynamic-update-slice_fusion), channel_id=1, source_target_pairs={{0,240},{16,0},{32,16},{48,32},{64,48},{80,64},{96,80},{112,96},{1... | collective-permute-start | bytes 1572872 | tf_op jit(solution)/shard_map/ppermute | solution.py:15
  15.9 0.8 copy-start.3
  47.6 1.0 copy-start.1
  65.2 0.7 copy-start.5
  107.9 10.9 %collective-permute-start.2 = (f32[2,2,128,256]{3,2,1,0:T(8,128)S(1)}, f32[2,2,128,256]{3,2,1,0:T(8,128)S(1)}, u32[]{:S(2)}, u32[]{:S(2)}) collective-permute-start(f32[2,2,128,256]{3,2,1,0:T(8,128)S(1)} %slice.169), channel_id=1, source_target_pairs={{0,16},{16,32},{32,48},{48,64},{64,80},{80,96},{96,112},{112,128},... | collective-permute-start | bytes 1572872 | tf_op jit(solution)/shard_map/ppermute | solution.py:15
  119.0 10.3 %copy-start = (f32[2,2,128,128]{3,2,1,0:T(8,128)S(1)}, f32[2,2,128,128]{3,2,1,0:T(8,128)}, u32[]{:S(2)}) copy-start(f32[2,2,128,128]{3,2,1,0:T(8,128)} %param.22) | copy-start | bytes 786436
  119.0 10.3 %collective-permute-start.3 = (f32[2,2,128,128]{3,2,1,0:T(8,128)S(1)}, f32[2,2,128,128]{3,2,1,0:T(8,128)S(1)}, u32[]{:S(2)}, u32[]{:S(2)}) collective-permute-start(f32[2,2,128,128]{3,2,1,0:T(8,128)S(1)} %slice.265), channel_id=1, source_target_pairs={{0,1},{1,2},{2,3},{3,4},{4,5},{5,6},{6,7},{7,8},{8,9},{9,10},{10,1... | collective-permute-start | bytes 786440 | tf_op jit(solution)/shard_map/ppermute | solution.py:15
  129.3 6.9 %collective-permute-start.4 = (f32[2,2,128,128]{3,2,1,0:T(8,128)S(1)}, f32[2,2,128,128]{3,2,1,0:T(8,128)S(1)}, u32[]{:S(2)}, u32[]{:S(2)}) collective-permute-start(f32[2,2,128,128]{3,2,1,0:T(8,128)S(1)} %fusion.39), channel_id=1, source_target_pairs={{0,15},{1,0},{2,1},{3,2},{4,3},{5,4},{6,5},{7,6},{8,7},{9,8},{10,9... | collective-permute-start | bytes 786440 | tf_op jit(solution)/shard_map/ppermute | solution.py:15
  136.2 9.4 %collective-permute-start.5 = (f32[2,2,128,256]{3,2,1,0:T(8,128)S(1)}, f32[2,2,128,256]{3,2,1,0:T(8,128)S(1)}, u32[]{:S(2)}, u32[]{:S(2)}) collective-permute-start(f32[2,2,128,256]{3,2,1,0:T(8,128)S(1)} %pad_maximum_fusion.2), channel_id=1, source_target_pairs={{0,240},{16,0},{32,16},{48,32},{64,48},{80,64},{96,80},{112,96},{1... | collective-permute-start | bytes 1572872 | tf_op jit(solution)/shard_map/ppermute | solution.py:15
  188.4 0.7 copy-start.4
  231.1 10.9 %collective-permute-start.6 = (f32[2,2,128,256]{3,2,1,0:T(8,128)S(1)}, f32[2,2,128,256]{3,2,1,0:T(8,128)S(1)}, u32[]{:S(2)}, u32[]{:S(2)}) collective-permute-start(f32[2,2,128,256]{3,2,1,0:T(8,128)S(1)} %slice.177), channel_id=1, source_target_pairs={{0,16},{16,32},{32,48},{48,64},{64,80},{80,96},{96,112},{112,128},... | collective-permute-start | bytes 1572872 | tf_op jit(solution)/shard_map/ppermute | solution.py:15
  242.2 10.1 %collective-permute-start.7 = (f32[2,2,128,128]{3,2,1,0:T(8,128)S(1)}, f32[2,2,128,128]{3,2,1,0:T(8,128)S(1)}, u32[]{:S(2)}, u32[]{:S(2)}) collective-permute-start(f32[2,2,128,128]{3,2,1,0:T(8,128)S(1)} %slice.267), channel_id=1, source_target_pairs={{0,1},{1,2},{2,3},{3,4},{4,5},{5,6},{6,7},{7,8},{8,9},{9,10},{10,1... | collective-permute-start | bytes 786440 | tf_op jit(solution)/shard_map/ppermute | solution.py:15
where the time goes:
time: 257 us; the launch traced here: 253 us
  matrix products  67.3 us (26%)
  local copies, waits for them, and re-layouts  63.1 us (25%)
  waiting for transfers between devices  61.1 us (24%)
  other arithmetic  43.6 us (17%)
  starting transfers between devices  15.5 us (6%)
    ppermute x8, waiting for transfers between devices, passed_along(): return lax.ppermute(value, axis, pairs)  61.1 us
    scatter-add x16, other arithmetic  42.3 us
    scatter-add x24, local copies, waits for them, and re-layouts  41.5 us
    gather x24, local copies, waits for them, and re-layouts  16.2 us
    ppermute x8, starting transfers between devices, passed_along(): return lax.ppermute(value, axis, pairs)  15.5 us
    dot_general x12, matrix products, transform(): jnp.einsum('ij,njk->nik', table_im, imag, precision=high)  8.81 us
    dot_general x12, matrix products, transform(): jnp.einsum('nij,jk->nik', left_im, table_im, precision=high)  8.71 us
    dot_general x12, matrix products, transform(): jnp.einsum('ij,njk->nik', table_re, real, precision=high)  8.44 us
  transfers between devices with their start and end apart: 8, of which 8 were waited for; matrix products, arithmetic and copies ran while one was open for 1% of the time, Pallas kernels for 0%

commit v1 on v0

v1 whole, which is shorter than its diff:
```python
import functools

import jax
import jax.numpy as jnp
import numpy as np
from jax import lax
from jax.experimental import pallas as pl
from jax.experimental.pallas import tpu as pltpu
from jax.sharding import PartitionSpec as P

ITERS = 2
STEP_RATE = 0.02
MESH = pl.DeviceIdType.MESH
N = 128
SLOTS = 4
PAIRS = 2

FR, FB, FD, GD, GB, GR = range(6)
FORWARD, INVERSE = 0, 1


def dft_tables():
    index = np.arange(N)
    angle = (index[:, None] * index[None, :] % N) * (-2.0 * np.pi / N)
    real, imag = np.cos(angle) / np.sqrt(N), np.sin(angle) / np.sqrt(N)
    right = np.block([[real, imag], [-imag, real]]).astype(np.float32)
    rights, lefts = [], []
    for table in (right, right.T):
        high = table.astype(jnp.bfloat16)
        low = (table - high.astype(np.float32)).astype(jnp.bfloat16)
        rights.append(np.concatenate([high, low, high], axis=0))
        lefts.append(np.concatenate([high.T, low.T, high.T], axis=1))
    return np.stack(rights), np.stack(lefts)


def split(value):
    high = value.astype(jnp.bfloat16)
    low = (value - high.astype(jnp.float32)).astype(jnp.bfloat16)
    return high, low


def kernel(
    axes,
    pos_ref,
    count_ref,
    obj_hbm,
    probe_ref,
    phase_ref,
    measured_hbm,
    rights_hbm,
    lefts_hbm,
    out_ref,
    ext0,
    ext1,
    win,
    wave,
    grad,
    in_corner,
    in_bottom,
    in_side,
    pad,
    measured,
    rights,
    lefts,
    prop,
    send_sem,
    recv_sem,
    local_sem,
):
    rows, cols = axes
    row, col = lax.axis_index("row"), lax.axis_index("col")
    left = (row, lax.rem(col + cols - 1, cols))
    right = (row, lax.rem(col + 1, cols))
    above = (lax.rem(row + rows - 1, rows), col)
    below = (lax.rem(row + 1, rows), col)
    exts = (ext0, ext1)

    barrier = pltpu.get_barrier_semaphore()
    for neighbour in (left, right, above, below):
        pl.semaphore_signal(barrier, inc=1, device_id=neighbour, device_id_type=MESH)

    def local(source, target, sem):
        return pltpu.make_async_copy(source, target, local_sem.at[sem])

    own_copies = [local(obj_hbm.at[s], exts[s].at[0, :, 0:N, :], s) for s in range(2)]
    table_copies = [local(rights_hbm, rights, 2), local(lefts_hbm, lefts, 3)]
    measured_copy = local(measured_hbm, measured, 4)
    for copy in own_copies + table_copies + [measured_copy]:
        copy.start()

    def remote(kind, s, source, target, device, c):
        return pltpu.make_async_remote_copy(
            src_ref=source,
            dst_ref=target,
            send_sem=send_sem.at[kind, s, c],
            recv_sem=recv_sem.at[kind, s, c],
            device_id=device,
            device_id_type=MESH,
        )

    def copies(kind, s, first=False):
        made = []
        for c in range(2):
            ext = exts[s]
            own = obj_hbm.at[s, c] if first else ext.at[0, c, 0:N, :]
            side = ext.at[1, c, 0:N, :]
            if kind == FR:
                args = (own, side, left)
            elif kind == FB:
                args = (own, ext.at[0, c, N : 2 * N, :], above)
            elif kind == FD:
                args = (side, ext.at[1, c, N : 2 * N, :], above)
            elif kind == GD:
                args = (grad.at[s, 3, c], in_corner.at[s, c], below)
            elif kind == GB:
                args = (grad.at[s, 2, c], in_bottom.at[s, c], below)
            else:
                args = (grad.at[s, 1, c], in_side.at[s, c], right)
            made.append(remote(kind, s, *args, c))
        return made

    lane = lax.broadcasted_iota(jnp.int32, (N, N), 1)

    def gather(s):
        ext = exts[s]
        for k in range(SLOTS):
            p, q = pos_ref[k, 0], pos_ref[k, 1]
            back = (N - q) & (N - 1)
            for c in range(2):
                near = ext[0, c, pl.ds(p, N), :]
                far = ext[1, c, pl.ds(p, N), :]
                mixed = pltpu.roll(jnp.where(lane >= q, near, far), back, 1)
                win[s, c, k // 2, :, (k % 2) * N : (k % 2 + 1) * N] = mixed

    def scatter_slot(k, c, value):
        q = pos_ref[k, 1]
        moved = pltpu.roll(value, q, 1)
        pad[k, 0, c, N : 2 * N, :] = jnp.where(lane >= q, moved, 0.0)
        pad[k, 1, c, N : 2 * N, :] = jnp.where(lane < q, moved, 0.0)

    def collect(s, quadrant):
        v, h = quadrant // 2, quadrant % 2
        for c in range(2):
            total = pad[0, h, c, pl.ds((v + 1) * N - pos_ref[0, 0], N), :]
            for k in range(1, SLOTS):
                total += pad[k, h, c, pl.ds((v + 1) * N - pos_ref[k, 0], N), :]
            grad[s, quadrant, c] = total

    def columns(re, im, which):
        high, low = split(jnp.concatenate([re, im], axis=0))
        stacked = jnp.concatenate([high, high, low], axis=0)
        out = jnp.dot(lefts[which], stacked, preferred_element_type=jnp.float32)
        return out[:N], out[N:]

    def lines(re, im, which):
        block = jnp.concatenate(
            [
                jnp.concatenate([re[:, :N], im[:, :N]], axis=1),
                jnp.concatenate([re[:, N:], im[:, N:]], axis=1),
            ],
            axis=0,
        )
        high, low = split(block)
        stacked = jnp.concatenate([high, high, low], axis=1)
        out = jnp.dot(stacked, rights[which], preferred_element_type=jnp.float32)
        return (
            jnp.concatenate([out[:N, :N], out[N:, :N]], axis=1),
            jnp.concatenate([out[:N, N:], out[N:, N:]], axis=1),
        )

    def twice(value):
        return jnp.concatenate([value, value], axis=1)

    pl.semaphore_wait(barrier, 4)
    started = {}

    def start(kind, s, first=False):
        started[kind, s] = copies(kind, s, first)
        for copy in started[kind, s]:
            copy.start()

    def wait_send(kind, s):
        for copy in started.pop((kind, s)):
            copy.wait_send()

    for s in range(2):
        start(FR, s, True)
        start(FB, s, True)

    prop[0] = jnp.cos(phase_ref[...])
    prop[1] = jnp.sin(phase_ref[...])
    zero = jnp.zeros((N, N), jnp.float32)
    for k in range(SLOTS):
        for h in range(2):
            for c in range(2):
                pad[k, h, c, 0:N, :] = zero
                pad[k, h, c, 2 * N : 3 * N, :] = zero
    for copy in own_copies + table_copies + [measured_copy]:
        copy.wait()

    def pass_on(s):
        arrived = started[FR, s]
        passed = copies(FD, s)
        for c in range(2):
            arrived[c].wait_recv()
            passed[c].start()
        started[FD, s] = passed

    def wait_recv(kind, s):
        for copy in started[kind, s]:
            copy.wait_recv()

    for step in range(ITERS):
        last = step == ITERS - 1
        order = (0, 1) if step == 0 else (1, 0)
        pass_on(order[0])
        pass_on(order[1])
        wait_recv(FB, 0)
        wait_recv(FD, 0)
        gather(0)

        for pair in range(PAIRS):
            p_re, p_im = twice(probe_ref[0]), twice(probe_ref[1])
            h_re, h_im = twice(prop[0]), twice(prop[1])
            o_re, o_im = win[0, 0, pair], win[0, 1, pair]
            re, im = p_re * o_re - p_im * o_im, p_re * o_im + p_im * o_re
            re, im = lines(re, im, FORWARD)
            re, im = columns(re, im, FORWARD)
            re, im = re * h_re - im * h_im, re * h_im + im * h_re
            re, im = columns(re, im, INVERSE)
            re, im = lines(re, im, INVERSE)
            wave[0, pair] = re
            wave[1, pair] = im

        wait_recv(FB, 1)
        wait_recv(FD, 1)
        gather(1)
        for pair in range(PAIRS):
            w_re, w_im = wave[0, pair], wave[1, pair]
            o_re, o_im = win[1, 0, pair], win[1, 1, pair]
            re, im = w_re * o_re - w_im * o_im, w_re * o_im + w_im * o_re
            re, im = lines(re, im, FORWARD)
            re, im = columns(re, im, FORWARD)
            seen = jnp.concatenate([measured[2 * pair], measured[2 * pair + 1]], axis=1)
            wide = lax.broadcasted_iota(jnp.int32, (N, 2 * N), 1)
            slot = jnp.where(wide < N, 2 * pair, 2 * pair + 1)
            factor = 2.0 * (re * re + im * im - seen)
            factor = jnp.where(slot < count_ref[0], factor, 0.0)
            re, im = columns(re * factor, im * factor, INVERSE)
            re, im = lines(re, im, INVERSE)
            g_re, g_im = w_re * re + w_im * im, w_re * im - w_im * re
            for half in range(2):
                k, part = 2 * pair + half, slice(half * N, (half + 1) * N)
                scatter_slot(k, 0, g_re[:, part])
                scatter_slot(k, 1, g_im[:, part])
            wave[0, pair] = o_re * re + o_im * im
            wave[1, pair] = o_re * im - o_im * re

        def send_back(s):
            for kind in (GD, GB, GR):
                if (kind, s) in started:
                    wait_send(kind, s)
            collect(s, 3)
            start(GD, s)
            collect(s, 2)
            start(GB, s)
            collect(s, 1)
            collect(s, 0)

        def add_corner(s):
            wait_send(FD, s)
            arrived, passed = started[GD, s], copies(GR, s)
            for c in range(2):
                arrived[c].wait_recv()
                grad[s, 1, c] = grad[s, 1, c] + in_corner[s, c]
                passed[c].start()
            started[GR, s] = passed

        def update(s):
            for kind in (FR, FB):
                if (kind, s) in started:
                    wait_send(kind, s)
            wait_recv(GB, s)
            arrived = started[GR, s]
            for c in range(2):
                arrived[c].wait_recv()
                total = grad[s, 0, c] + in_bottom[s, c] + in_side[s, c]
                new = exts[s][0, c, 0:N, :] - STEP_RATE * total
                if last:
                    out_ref[s, c] = new
                else:
                    exts[s][0, c, 0:N, :] = new
            if not last:
                start(FR, s)
                start(FB, s)

        send_back(1)

        def back(pair):
            h_re, h_im = twice(prop[0]), twice(prop[1])
            re, im = wave[0, pair], wave[1, pair]
            re, im = lines(re, im, FORWARD)
            re, im = columns(re, im, FORWARD)
            re, im = h_re * re + h_im * im, h_re * im - h_im * re
            re, im = columns(re, im, INVERSE)
            re, im = lines(re, im, INVERSE)
            p_re, p_im = twice(probe_ref[0]), twice(probe_ref[1])
            g_re, g_im = p_re * re + p_im * im, p_re * im - p_im * re
            for half in range(2):
                k, part = 2 * pair + half, slice(half * N, (half + 1) * N)
                scatter_slot(k, 0, g_re[:, part])
                scatter_slot(k, 1, g_im[:, part])

        back(0)
        add_corner(1)
        back(1)
        send_back(0)
        update(1)
        add_corner(0)
        update(0)

    for kind, s in list(started):
        wait_send(kind, s)


def per_device(object_slices, probe, phase, positions, counts, measured):
    rights, lefts = dft_tables()
    vmem = pl.BlockSpec(memory_space=pltpu.VMEM)
    smem = pl.BlockSpec(memory_space=pltpu.SMEM)
    anywhere = pl.BlockSpec(memory_space=pl.ANY)
    f32 = jnp.float32
    return pl.pallas_call(
        functools.partial(kernel, (lax.axis_size("row"), lax.axis_size("col"))),
        out_shape=jax.ShapeDtypeStruct((2, 2, N, N), f32),
        in_specs=[smem, smem, anywhere, vmem, vmem, anywhere, anywhere, anywhere],
        out_specs=vmem,
        scratch_shapes=[
            pltpu.VMEM((2, 2, 2 * N, N), f32),
            pltpu.VMEM((2, 2, 2 * N, N), f32),
            pltpu.VMEM((2, 2, PAIRS, N, 2 * N), f32),
            pltpu.VMEM((2, PAIRS, N, 2 * N), f32),
            pltpu.VMEM((2, 4, 2, N, N), f32),
            pltpu.VMEM((2, 2, N, N), f32),
            pltpu.VMEM((2, 2, N, N), f32),
            pltpu.VMEM((2, 2, N, N), f32),
            pltpu.VMEM((SLOTS, 2, 2, 3 * N, N), f32),
            pltpu.VMEM((SLOTS, N, N), f32),
            pltpu.VMEM((2, 6 * N, 2 * N), jnp.bfloat16),
            pltpu.VMEM((2, 2 * N, 6 * N), jnp.bfloat16),
            pltpu.VMEM((2, N, N), f32),
            pltpu.SemaphoreType.DMA((6, 2, 2)),
            pltpu.SemaphoreType.DMA((6, 2, 2)),
            pltpu.SemaphoreType.DMA((5,)),
        ],
        compiler_params=pltpu.CompilerParams(
            collective_id=0, has_side_effects=True, vmem_limit_bytes=56 * 1024 * 1024
        ),
        cost_estimate=pl.CostEstimate(
            flops=6 * 805306368, bytes_accessed=2500000, transcendentals=0
        ),
    )(
        positions.reshape(SLOTS, 2),
        counts.reshape(1),
        object_slices,
        probe,
        phase,
        measured.reshape(SLOTS, N, N),
        jnp.asarray(rights),
        jnp.asarray(lefts),
    )


def solution(mesh):
    return jax.shard_map(
        per_device,
        mesh=mesh,
        in_specs=(
            P(None, None, "row", "col"),
            P(),
            P(),
            P("row", "col", None, None),
            P("row", "col"),
            P("row", "col", None, None, None),
        ),
        out_specs=P(None, None, "row", "col"),
        check_vma=False,
    )
```

time: 257 us -> 74.2 us (0.29); the launches traced: 253 us -> 73.2 us
  Pallas kernels: 0 us -> 69.5 us
  matrix products: 67.3 us -> 0 us
  waiting for transfers between devices: 61.1 us -> 0 us
  local copies, waits for them, and re-layouts: 63.1 us -> 3.01 us
  other arithmetic: 43.6 us -> 0 us
  starting transfers between devices: 15.5 us -> 0 us
    pallas_call x0 -> x1, Pallas kernels: none -> 69.5 us  [per_device(): pl.pallas_call(functools.partial(kernel, (lax.axis_size('row'), lax.axis_...]
    dot_general x96 -> x0, matrix products: 67.3 us -> none  [the longest x12 8.81 us: transform(): jnp.einsum('ij,njk->nik', table_im, imag, precision=high)]
    ppermute x8 -> x0, waiting for transfers between devices: 61.1 us -> none  [passed_along(): return lax.ppermute(value, axis, pairs)]
    scatter-add x16 -> x0, other arithmetic: 42.3 us -> none
    scatter-add x24 -> x0, local copies, waits for them, and re-layouts: 41.5 us -> none
    gather x24 -> x0, local copies, waits for them, and re-layouts: 16.2 us -> none
    ppermute x8 -> x0, starting transfers between devices: 15.5 us -> none  [passed_along(): return lax.ppermute(value, axis, pairs)]
  transfers between devices with their start and end apart: 8 -> 0, of which waited for: 8 -> 0; matrix products, arithmetic and copies ran while one was open for 1% -> 0% of each run, Pallas kernels for 0% -> 0%
where the time goes in v1:
time: 74.2 us; the launch traced here: 73.2 us
  Pallas kernels  69.5 us (94%)
  local copies, waits for them, and re-layouts  3.01 us (4%)
    pallas_call x1, Pallas kernels, per_device(): pl.pallas_call(functools.partial(kernel, (lax.axis_size('row'), lax.axis_...  69.5 us
    unnamed x3, local copies, waits for them, and re-layouts  2.34 us

profile of v1, /device:TPU:2, one launch (start us, length us, event | category | flops | bytes accessed | tf_op | source)
XLA Modules:
  0.0 73.2 jit_solution(8262083751504224782)
XLA Ops:
  0.7 0.0 copy-start
  0.7 0.7 copy-done
  1.3 0.7 copy.9.pos_ref
  2.0 69.5 %shard_map.82 = f32[2,2,128,128]{3,2,1,0:T(8,128)} custom-call(s32[4,2]{1,0:T(4,128)} %copy.9.pos_ref, s32[1]{0:T(128)} %bitcast.3.count_ref, f32[2,2,128,128]{3,2,1,0:T(8,128)} %obj_hbm.1, f32[2,128,128]{2,1,0:T(8,128)} %probe_ref.1, f32[128,128]{1,0:T(8,128)} %phase_ref.1, f32[4,128,128]{2,1,0:T(8,128)} %bitcast.5, ...), custom_call_target="tpu_custom_call" | custom-call | flops 4831838208 | bytes 2500000 | tf_op jit(solution)/shard_map/pallas_call | solution.py:332
  71.5 1.7 %copy.12 = f32[2,2,128,128]{3,2,1,0:T(8,128)} copy(f32[2,2,128,128]{3,2,1,0:T(8,128)} %shard_map.82) | data formatting | bytes 524288
Async XLA Ops:
  0.7 0.7 copy-start

commit v2 on v1

--- a/solution.py
+++ b/solution.py
@@ -15,7 +15,8 @@
 SLOTS = 4
 PAIRS = 2
 
-FR, FB, FD, GD, GB, GR = range(6)
+FR, FB, FD, GD, GB, GR, FE, GE = range(8)
+RUN = 8
 FORWARD, INVERSE = 0, 1
 
 
@@ -41,11 +42,11 @@
 
 def kernel(
     axes,
-    pos_ref,
-    count_ref,
+    pos_hbm,
+    count_hbm,
     obj_hbm,
-    probe_ref,
-    phase_ref,
+    probe_hbm,
+    phase_hbm,
     measured_hbm,
     rights_hbm,
     lefts_hbm,
@@ -58,7 +59,12 @@
     in_corner,
     in_bottom,
     in_side,
+    in_extra,
     pad,
+    positions,
+    counts,
+    probe_ref,
+    phase_ref,
     measured,
     rights,
     lefts,
@@ -82,49 +88,62 @@
     def local(source, target, sem):
         return pltpu.make_async_copy(source, target, local_sem.at[sem])
 
+    small_copies = [
+        local(pos_hbm, positions, 5),
+        local(count_hbm, counts, 6),
+        local(probe_hbm, probe_ref, 7),
+        local(phase_hbm, phase_ref, 8),
+    ]
     own_copies = [local(obj_hbm.at[s], exts[s].at[0, :, 0:N, :], s) for s in range(2)]
     table_copies = [local(rights_hbm, rights, 2), local(lefts_hbm, lefts, 3)]
     measured_copy = local(measured_hbm, measured, 4)
-    for copy in own_copies + table_copies + [measured_copy]:
+    argument_copies = small_copies + own_copies + table_copies + [measured_copy]
+    for copy in argument_copies:
         copy.start()
 
-    def remote(kind, s, source, target, device, c):
+    row_end, row_start = lax.rem(row, RUN) == RUN - 1, lax.rem(row, RUN) == 0
+    col_end, col_start = lax.rem(col, RUN) == RUN - 1, lax.rem(col, RUN) == 0
+    passes_up = jnp.logical_not(row_start & col_end)
+    passes_left = row_end & col_start
+    corner_down = jnp.logical_not(row_end & col_start)
+    corner_right = row_end & col_start
+    corner_from_above = jnp.logical_not(row_start & col_start)
+    corner_from_left = row_end & (lax.rem(col, RUN) == 1)
+
+    def piece(kind, s, c, first=False):
+        ext = exts[s]
+        own = obj_hbm.at[s, c] if first else ext.at[0, c, 0:N, :]
+        side, bottom = ext.at[1, c, 0:N, :], ext.at[0, c, N : 2 * N, :]
+        corner = ext.at[1, c, N : 2 * N, :]
+        source, target, device = {
+            FR: (own, side, left),
+            FB: (own, bottom, above),
+            FD: (side, corner, above),
+            FE: (bottom, corner, left),
+            GD: (grad.at[s, 3, c], in_corner.at[s, c], below),
+            GE: (grad.at[s, 3, c], in_extra.at[s, c], right),
+            GB: (grad.at[s, 2, c], in_bottom.at[s, c], below),
+            GR: (grad.at[s, 1, c], in_side.at[s, c], right),
+        }[kind]
+        landing = FD if kind == FE else kind
         return pltpu.make_async_remote_copy(
             src_ref=source,
             dst_ref=target,
             send_sem=send_sem.at[kind, s, c],
-            recv_sem=recv_sem.at[kind, s, c],
+            recv_sem=recv_sem.at[landing, s, c],
             device_id=device,
             device_id_type=MESH,
         )
 
     def copies(kind, s, first=False):
-        made = []
-        for c in range(2):
-            ext = exts[s]
-            own = obj_hbm.at[s, c] if first else ext.at[0, c, 0:N, :]
-            side = ext.at[1, c, 0:N, :]
-            if kind == FR:
-                args = (own, side, left)
-            elif kind == FB:
-                args = (own, ext.at[0, c, N : 2 * N, :], above)
-            elif kind == FD:
-                args = (side, ext.at[1, c, N : 2 * N, :], above)
-            elif kind == GD:
-                args = (grad.at[s, 3, c], in_corner.at[s, c], below)
-            elif kind == GB:
-                args = (grad.at[s, 2, c], in_bottom.at[s, c], below)
-            else:
-                args = (grad.at[s, 1, c], in_side.at[s, c], right)
-            made.append(remote(kind, s, *args, c))
-        return made
+        return (piece(kind, s, c, first) for c in range(2))
 
     lane = lax.broadcasted_iota(jnp.int32, (N, N), 1)
 
     def gather(s):
         ext = exts[s]
         for k in range(SLOTS):
-            p, q = pos_ref[k, 0], pos_ref[k, 1]
+            p, q = positions[0, 0, 0, k], positions[0, 0, 1, k]
             back = (N - q) & (N - 1)
             for c in range(2):
                 near = ext[0, c, pl.ds(p, N), :]
@@ -133,7 +152,7 @@
                 win[s, c, k // 2, :, (k % 2) * N : (k % 2 + 1) * N] = mixed
 
     def scatter_slot(k, c, value):
-        q = pos_ref[k, 1]
+        q = positions[0, 0, 1, k]
         moved = pltpu.roll(value, q, 1)
         pad[k, 0, c, N : 2 * N, :] = jnp.where(lane >= q, moved, 0.0)
         pad[k, 1, c, N : 2 * N, :] = jnp.where(lane < q, moved, 0.0)
@@ -141,9 +160,9 @@
     def collect(s, quadrant):
         v, h = quadrant // 2, quadrant % 2
         for c in range(2):
-            total = pad[0, h, c, pl.ds((v + 1) * N - pos_ref[0, 0], N), :]
+            total = pad[0, h, c, pl.ds((v + 1) * N - positions[0, 0, 0, 0], N), :]
             for k in range(1, SLOTS):
-                total += pad[k, h, c, pl.ds((v + 1) * N - pos_ref[k, 0], N), :]
+                total += pad[k, h, c, pl.ds((v + 1) * N - positions[0, 0, 0, k], N), :]
             grad[s, quadrant, c] = total
 
     def columns(re, im, which):
@@ -172,21 +191,29 @@
         return jnp.concatenate([value, value], axis=1)
 
     pl.semaphore_wait(barrier, 4)
-    started = {}
+    first_sent = set()
 
     def start(kind, s, first=False):
-        started[kind, s] = copies(kind, s, first)
-        for copy in started[kind, s]:
+        if first:
+            first_sent.add((kind, s))
+        for copy in copies(kind, s, first):
             copy.start()
 
     def wait_send(kind, s):
-        for copy in started.pop((kind, s)):
+        first = (kind, s) in first_sent
+        first_sent.discard((kind, s))
+        for copy in copies(kind, s, first):
             copy.wait_send()
 
-    for s in range(2):
-        start(FR, s, True)
-        start(FB, s, True)
-
+    def wait_recv(kind, s):
+        for copy in copies(kind, s):
+            copy.wait_recv()
+
+    start(FR, 0, True)
+    start(FB, 0, True)
+
+    for copy in argument_copies:
+        copy.wait()
     prop[0] = jnp.cos(phase_ref[...])
     prop[1] = jnp.sin(phase_ref[...])
     zero = jnp.zeros((N, N), jnp.float32)
@@ -195,29 +222,39 @@
             for c in range(2):
                 pad[k, h, c, 0:N, :] = zero
                 pad[k, h, c, 2 * N : 3 * N, :] = zero
-    for copy in own_copies + table_copies + [measured_copy]:
-        copy.wait()
+
+    wait_send(FB, 0)
+    start(FB, 1, True)
+    wait_send(FR, 0)
+    start(FR, 1, True)
 
     def pass_on(s):
-        arrived = started[FR, s]
-        passed = copies(FD, s)
         for c in range(2):
-            arrived[c].wait_recv()
-            passed[c].start()
-        started[FD, s] = passed
-
-    def wait_recv(kind, s):
-        for copy in started[kind, s]:
-            copy.wait_recv()
+            piece(FR, s, c).wait_recv()
+
+            @pl.when(passes_up)
+            def _():
+                piece(FD, s, c).start()
+
+        for c in range(2):
+            piece(FB, s, c).wait_recv()
+
+            @pl.when(passes_left)
+            def _():
+                piece(FE, s, c).start()
 
     for step in range(ITERS):
         last = step == ITERS - 1
-        order = (0, 1) if step == 0 else (1, 0)
-        pass_on(order[0])
-        pass_on(order[1])
-        wait_recv(FB, 0)
-        wait_recv(FD, 0)
-        gather(0)
+        if step == 0:
+            pass_on(0)
+            wait_recv(FD, 0)
+            gather(0)
+            pass_on(1)
+        else:
+            pass_on(1)
+            pass_on(0)
+            wait_recv(FD, 0)
+            gather(0)
 
         for pair in range(PAIRS):
             p_re, p_im = twice(probe_ref[0]), twice(probe_ref[1])
@@ -232,7 +269,6 @@
             wave[0, pair] = re
             wave[1, pair] = im
 
-        wait_recv(FB, 1)
         wait_recv(FD, 1)
         gather(1)
         for pair in range(PAIRS):
@@ -245,7 +281,7 @@
             wide = lax.broadcasted_iota(jnp.int32, (N, 2 * N), 1)
             slot = jnp.where(wide < N, 2 * pair, 2 * pair + 1)
             factor = 2.0 * (re * re + im * im - seen)
-            factor = jnp.where(slot < count_ref[0], factor, 0.0)
+            factor = jnp.where(slot < counts[0, 0], factor, 0.0)
             re, im = columns(re * factor, im * factor, INVERSE)
             re, im = lines(re, im, INVERSE)
             g_re, g_im = w_re * re + w_im * im, w_re * im - w_im * re
@@ -257,33 +293,67 @@
             wave[1, pair] = o_re * im - o_im * re
 
         def send_back(s):
-            for kind in (GD, GB, GR):
-                if (kind, s) in started:
-                    wait_send(kind, s)
+            @pl.when(passes_up)
+            def _():
+                wait_send(FD, s)
+
+            @pl.when(passes_left)
+            def _():
+                wait_send(FE, s)
+
             collect(s, 3)
-            start(GD, s)
+
+            @pl.when(corner_down)
+            def _():
+                start(GD, s)
+
+            @pl.when(corner_right)
+            def _():
+                start(GE, s)
+
             collect(s, 2)
-            start(GB, s)
+
+            @pl.when(jnp.logical_not(corner_from_left))
+            def _():
+                start(GB, s)
+
             collect(s, 1)
             collect(s, 0)
 
+            @pl.when(corner_from_left)
+            def _():
+                for c in range(2):
+                    piece(GE, s, c).wait_recv()
+                    grad[s, 2, c] = grad[s, 2, c] + in_extra[s, c]
+                    piece(GB, s, c).start()
+
         def add_corner(s):
-            wait_send(FD, s)
-            arrived, passed = started[GD, s], copies(GR, s)
             for c in range(2):
-                arrived[c].wait_recv()
-                grad[s, 1, c] = grad[s, 1, c] + in_corner[s, c]
-                passed[c].start()
-            started[GR, s] = passed
+
+                @pl.when(corner_from_above)
+                def _():
+                    piece(GD, s, c).wait_recv()
+                    grad[s, 1, c] = grad[s, 1, c] + in_corner[s, c]
+
+                piece(GR, s, c).start()
 
         def update(s):
-            for kind in (FR, FB):
-                if (kind, s) in started:
-                    wait_send(kind, s)
-            wait_recv(GB, s)
-            arrived = started[GR, s]
+            @pl.when(corner_down)
+            def _():
+                wait_send(GD, s)
+
+            @pl.when(corner_right)
+            def _():
+                wait_send(GE, s)
+
+            wait_send(GB, s)
+            wait_send(GR, s)
+            if step > 0 or s == 1:
+                wait_send(FR, s)
+                wait_send(FB, s)
             for c in range(2):
-                arrived[c].wait_recv()
+                piece(GB, s, c).wait_recv()
+                piece(GR, s, c).wait_recv()
                 total = grad[s, 0, c] + in_bottom[s, c] + in_side[s, c]
                 new = exts[s][0, c, 0:N, :] - STEP_RATE * total
                 if last:
@@ -315,24 +385,20 @@
         add_corner(1)
         back(1)
         send_back(0)
+        add_corner(0)
         update(1)
-        add_corner(0)
         update(0)
-
-    for kind, s in list(started):
-        wait_send(kind, s)
 
 
 def per_device(object_slices, probe, phase, positions, counts, measured):
     rights, lefts = dft_tables()
     vmem = pl.BlockSpec(memory_space=pltpu.VMEM)
-    smem = pl.BlockSpec(memory_space=pltpu.SMEM)
-    anywhere = pl.BlockSpec(memory_space=pl.ANY)
+    hbm = pl.BlockSpec(memory_space=pltpu.HBM)
     f32 = jnp.float32
     return pl.pallas_call(
         functools.partial(kernel, (lax.axis_size("row"), lax.axis_size("col"))),
         out_shape=jax.ShapeDtypeStruct((2, 2, N, N), f32),
-        in_specs=[smem, smem, anywhere, vmem, vmem, anywhere, anywhere, anywhere],
+        in_specs=[hbm] * 8,
         out_specs=vmem,
         scratch_shapes=[
             pltpu.VMEM((2, 2, 2 * N, N), f32),
@@ -343,14 +409,19 @@
             pltpu.VMEM((2, 2, N, N), f32),
             pltpu.VMEM((2, 2, N, N), f32),
             pltpu.VMEM((2, 2, N, N), f32),
+            pltpu.VMEM((2, 2, N, N), f32),
             pltpu.VMEM((SLOTS, 2, 2, 3 * N, N), f32),
+            pltpu.SMEM((1, 1, 2, SLOTS), jnp.int32),
+            pltpu.SMEM((1, 1), jnp.int32),
+            pltpu.VMEM((2, N, N), f32),
+            pltpu.VMEM((N, N), f32),
             pltpu.VMEM((SLOTS, N, N), f32),
             pltpu.VMEM((2, 6 * N, 2 * N), jnp.bfloat16),
             pltpu.VMEM((2, 2 * N, 6 * N), jnp.bfloat16),
             pltpu.VMEM((2, N, N), f32),
-            pltpu.SemaphoreType.DMA((6, 2, 2)),
-            pltpu.SemaphoreType.DMA((6, 2, 2)),
-            pltpu.SemaphoreType.DMA((5,)),
+            pltpu.SemaphoreType.DMA((8, 2, 2)),
+            pltpu.SemaphoreType.DMA((8, 2, 2)),
+            pltpu.SemaphoreType.DMA((9,)),
         ],
         compiler_params=pltpu.CompilerParams(
             collective_id=0, has_side_effects=True, vmem_limit_bytes=56 * 1024 * 1024
@@ -359,8 +430,8 @@
             flops=6 * 805306368, bytes_accessed=2500000, transcendentals=0
         ),
     )(
-        positions.reshape(SLOTS, 2),
-        counts.reshape(1),
+        positions.transpose(0, 1, 3, 2),
+        counts,
         object_slices,
         probe,
         phase,

time: 74.2 us -> 72 us (0.970)
  the two profiles are of different devices: /device:TPU:2 before, /device:TPU:1 now
where the time goes in v2:
time: 72 us; the launch traced here: 71.9 us
  Pallas kernels  69.5 us (97%)
  local copies, waits for them, and re-layouts  1.67 us (2%)
    pallas_call x1, Pallas kernels, per_device(): pl.pallas_call(functools.partial(kernel, (lax.axis_size('row'), lax.axis_...  69.5 us
    unnamed x1, local copies, waits for them, and re-layouts  1.67 us

profile of v2, /device:TPU:1, one launch (start us, length us, event | category | flops | bytes accessed | tf_op | source)
XLA Modules:
  0.0 71.9 jit_solution(9675955629636800541)
XLA Ops:
  0.7 69.5 %shard_map.82 = f32[2,2,128,128]{3,2,1,0:T(8,128)} custom-call(s32[1,1,2,4]{3,2,1,0:T(2,128)} %bitcast.3, s32[1,1]{1,0:T(1,128)S(6)} %copy.10.count_hbm, f32[2,2,128,128]{3,2,1,0:T(8,128)} %obj_hbm.1, f32[2,128,128]{2,1,0:T(8,128)} %probe_hbm.1, f32[128,128]{1,0:T(8,128)} %phase_hbm.1, f32[4,128,128]{2,1,0:T(8,128)} %bitcast.2, ...), custom_call_target="tpu_custom_call" | custom-call | flops 4831838208 | bytes 2500000 | tf_op jit(solution)/shard_map/pallas_call | solution.py:398
  70.2 1.7 %copy.11 = f32[2,2,128,128]{3,2,1,0:T(8,128)} copy(f32[2,2,128,128]{3,2,1,0:T(8,128)} %shard_map.82) | data formatting | bytes 524288

commit v3 on v2

v3 whole, which is shorter than its diff:
```python
import functools

import jax
import jax.numpy as jnp
import numpy as np
from jax import lax
from jax.experimental import pallas as pl
from jax.experimental.pallas import tpu as pltpu
from jax.sharding import PartitionSpec as P

ITERS = 2
STEP_RATE = 0.02
MESH = pl.DeviceIdType.MESH
N = 128
SLOTS = 4

FR, FB, FD, GD, GB, GR, FE, GE = range(8)
RUN = 8
FORWARD, INVERSE = 0, 1


def dft_tables():
    index = np.arange(N)
    angle = (index[:, None] * index[None, :] % N) * (-2.0 * np.pi / N)
    real, imag = np.cos(angle) / np.sqrt(N), np.sin(angle) / np.sqrt(N)
    right = np.block([[real, imag], [-imag, real]]).astype(np.float32)
    rights, lefts = [], []
    for table in (right, right.T):
        high = table.astype(jnp.bfloat16)
        low = (table - high.astype(np.float32)).astype(jnp.bfloat16)
        rights.append(np.concatenate([high, low, high], axis=0))
        lefts.append(np.concatenate([high.T, low.T, high.T], axis=1))
    return np.stack(rights), np.stack(lefts)


def split(value):
    high = value.astype(jnp.bfloat16)
    low = (value - high.astype(jnp.float32)).astype(jnp.bfloat16)
    return high, low


def kernel(
    axes,
    pos_hbm,
    count_hbm,
    obj_hbm,
    probe_hbm,
    phase_hbm,
    measured_hbm,
    rights_hbm,
    lefts_hbm,
    out_ref,
    ext0,
    ext1,
    win,
    wave,
    grad,
    in_corner,
    in_bottom,
    in_side,
    in_extra,
    in_right,
    partly,
    pad,
    positions,
    counts,
    probe_ref,
    phase_ref,
    measured,
    rights,
    lefts,
    prop,
    send_sem,
    recv_sem,
    local_sem,
):
    rows, cols = axes
    row, col = lax.axis_index("row"), lax.axis_index("col")
    left = (row, lax.rem(col + cols - 1, cols))
    right = (row, lax.rem(col + 1, cols))
    above = (lax.rem(row + rows - 1, rows), col)
    below = (lax.rem(row + 1, rows), col)
    exts = (ext0, ext1)

    barrier = pltpu.get_barrier_semaphore()
    for neighbour in (left, right, above, below):
        pl.semaphore_signal(barrier, inc=1, device_id=neighbour, device_id_type=MESH)

    def local(source, target, sem):
        return pltpu.make_async_copy(source, target, local_sem.at[sem])

    small_copies = [
        local(pos_hbm, positions, 5),
        local(count_hbm, counts, 6),
        local(probe_hbm, probe_ref, 7),
        local(phase_hbm, phase_ref, 8),
    ]
    own_copies = [local(obj_hbm.at[s], exts[s].at[0, :, 0:N, :], s) for s in range(2)]
    table_copies = [local(rights_hbm, rights, 2), local(lefts_hbm, lefts, 3)]
    measured_copy = local(measured_hbm, measured, 4)
    argument_copies = small_copies + own_copies + table_copies + [measured_copy]
    for copy in argument_copies:
        copy.start()

    row_end, row_start = lax.rem(row, RUN) == RUN - 1, lax.rem(row, RUN) == 0
    col_end, col_start = lax.rem(col, RUN) == RUN - 1, lax.rem(col, RUN) == 0
    passes_up = jnp.logical_not(row_start & col_end)
    passes_left = row_end & col_start
    corner_down = jnp.logical_not(row_end & col_start)
    corner_right = row_end & col_start
    corner_from_above = jnp.logical_not(row_start & col_start)
    corner_from_left = row_end & (lax.rem(col, RUN) == 1)

    def piece(step, kind, s, c):
        ext = exts[s]
        side, bottom = ext.at[1, c, 0:N, :], ext.at[0, c, N : 2 * N, :]
        corner, own = ext.at[1, c, N : 2 * N, :], ext.at[0, c, 0:N, :]
        source, target, device = {
            FR: (partly.at[s, c], in_right.at[s, c], left)
            if step
            else (obj_hbm.at[s, c], side, left),
            FB: (own if step else obj_hbm.at[s, c], bottom, above),
            FD: (side, corner, above),
            FE: (bottom, corner, left),
            GD: (grad.at[step, s, 3, c], in_corner.at[step, s, c], below),
            GE: (grad.at[step, s, 3, c], in_extra.at[step, s, c], right),
            GB: (grad.at[step, s, 2, c], in_bottom.at[step, s, c], below),
            GR: (grad.at[step, s, 1, c], in_side.at[step, s, c], right),
        }[kind]
        landing = FD if kind == FE else kind
        return pltpu.make_async_remote_copy(
            src_ref=source,
            dst_ref=target,
            send_sem=send_sem.at[step, kind, s, c],
            recv_sem=recv_sem.at[step, landing, s, c],
            device_id=device,
            device_id_type=MESH,
        )

    def start(step, kind, s):
        for c in range(2):
            piece(step, kind, s, c).start()

    def wait_send(step, kind, s):
        for c in range(2):
            piece(step, kind, s, c).wait_send()

    def wait_recv(step, kind, s):
        for c in range(2):
            piece(step, kind, s, c).wait_recv()

    lane = lax.broadcasted_iota(jnp.int32, (N, N), 1)

    def gather(s):
        ext = exts[s]
        for k in range(SLOTS):
            p, q = positions[0, 0, 0, k], positions[0, 0, 1, k]
            back = (N - q) & (N - 1)
            for c in range(2):
                near = ext[0, c, pl.ds(p, N), :]
                far = ext[1, c, pl.ds(p, N), :]
                mixed = pltpu.roll(jnp.where(lane >= q, near, far), back, 1)
                win[s, c, :, k * N : (k + 1) * N] = mixed

    def scatter_slot(k, c, value):
        q = positions[0, 0, 1, k]
        moved = pltpu.roll(value, q, 1)
        pad[k, 0, c, N : 2 * N, :] = jnp.where(lane >= q, moved, 0.0)
        pad[k, 1, c, N : 2 * N, :] = jnp.where(lane < q, moved, 0.0)

    def collect(step, s, quadrant):
        v, h = quadrant // 2, quadrant % 2
        for c in range(2):
            total = pad[0, h, c, pl.ds((v + 1) * N - positions[0, 0, 0, 0], N), :]
            for k in range(1, SLOTS):
                total += pad[k, h, c, pl.ds((v + 1) * N - positions[0, 0, 0, k], N), :]
            grad[step, s, quadrant, c] = total

    def columns(re, im, which):
        high, low = split(jnp.concatenate([re, im], axis=0))
        stacked = jnp.concatenate([high, high, low], axis=0)
        out = jnp.dot(lefts[which], stacked, preferred_element_type=jnp.float32)
        return out[:N], out[N:]

    def lines(re, im, which):
        block = jnp.concatenate(
            [
                jnp.concatenate([re[:, part], im[:, part]], axis=1)
                for part in (slice(k * N, (k + 1) * N) for k in range(SLOTS))
            ],
            axis=0,
        )
        high, low = split(block)
        stacked = jnp.concatenate([high, high, low], axis=1)
        out = jnp.dot(stacked, rights[which], preferred_element_type=jnp.float32)
        return tuple(
            jnp.concatenate(
                [out[k * N : (k + 1) * N, part] for k in range(SLOTS)], axis=1
            )
            for part in (slice(0, N), slice(N, 2 * N))
        )

    def for_all(value):
        return jnp.concatenate([value] * SLOTS, axis=1)

    def scatter(re, im):
        for k in range(SLOTS):
            scatter_slot(k, 0, re[:, k * N : (k + 1) * N])
            scatter_slot(k, 1, im[:, k * N : (k + 1) * N])

    pl.semaphore_wait(barrier, 4)
    start(0, FR, 0)
    start(0, FB, 0)

    for copy in argument_copies:
        copy.wait()
    prop[0] = jnp.cos(phase_ref[...])
    prop[1] = jnp.sin(phase_ref[...])
    zero = jnp.zeros((N, N), jnp.float32)
    for k in range(SLOTS):
        for h in range(2):
            for c in range(2):
                pad[k, h, c, 0:N, :] = zero
                pad[k, h, c, 2 * N : 3 * N, :] = zero

    wait_send(0, FB, 0)
    start(0, FB, 1)
    wait_send(0, FR, 0)
    start(0, FR, 1)

    def pass_side_up(step, s, c):
        @pl.when(passes_up)
        def _():
            piece(step, FD, s, c).start()

    def take_bottom(step, s):
        for c in range(2):
            piece(step, FB, s, c).wait_recv()

            @pl.when(passes_left)
            def _():
                piece(step, FE, s, c).start()

    def first_halo(s):
        for c in range(2):
            piece(0, FR, s, c).wait_recv()
            pass_side_up(0, s, c)
        take_bottom(0, s)

    def send_back(step, s):
        if step == 0:
            @pl.when(passes_up)
            def _():
                wait_send(0, FD, s)

            @pl.when(passes_left)
            def _():
                wait_send(0, FE, s)

        collect(step, s, 3)

        @pl.when(corner_down)
        def _():
            start(step, GD, s)

        @pl.when(corner_right)
        def _():
            start(step, GE, s)

        collect(step, s, 2)

        @pl.when(jnp.logical_not(corner_from_left))
        def _():
            start(step, GB, s)

        collect(step, s, 1)
        collect(step, s, 0)

        @pl.when(corner_from_left)
        def _():
            for c in range(2):
                piece(step, GE, s, c).wait_recv()
                grad[step, s, 2, c] = grad[step, s, 2, c] + in_extra[step, s, c]
                piece(step, GB, s, c).start()

    def send_side(step, s):
        for c in range(2):

            @pl.when(corner_from_above)
            def _():
                piece(step, GD, s, c).wait_recv()
                grad[step, s, 1, c] = grad[step, s, 1, c] + in_corner[step, s, c]

            piece(step, GR, s, c).start()

    def send_partly(step, s):
        for c in range(2):
            piece(step, GB, s, c).wait_recv()
            total = grad[step, s, 0, c] + in_bottom[step, s, c]
            new = exts[s][0, c, 0:N, :] - STEP_RATE * total
            if step == ITERS - 1:
                out_ref[s, c] = new
            else:
                partly[s, c] = new
                piece(step + 1, FR, s, c).start()

    def finish(step, s):
        for c in range(2):
            piece(step, GR, s, c).wait_recv()
            if step == ITERS - 1:
                out_ref[s, c] = out_ref[s, c] - STEP_RATE * in_side[step, s, c]
            else:
                new = partly[s, c] - STEP_RATE * in_side[step, s, c]
                exts[s][0, c, 0:N, :] = new
                piece(step + 1, FB, s, c).start()
                piece(step + 1, FR, s, c).wait_recv()
                exts[s][1, c, 0:N, :] = in_right[s, c] - STEP_RATE * grad[step, s, 1, c]
                pass_side_up(step + 1, s, c)

    for step in range(ITERS):
        if step == 0:
            first_halo(0)
        else:
            take_bottom(step, 0)
        wait_recv(step, FD, 0)
        gather(0)
        if step == 0:
            first_halo(1)

        p_re, p_im = for_all(probe_ref[0]), for_all(probe_ref[1])
        h_re, h_im = for_all(prop[0]), for_all(prop[1])
        o_re, o_im = win[0, 0], win[0, 1]
        re, im = p_re * o_re - p_im * o_im, p_re * o_im + p_im * o_re
        re, im = lines(re, im, FORWARD)
        re, im = columns(re, im, FORWARD)
        re, im = re * h_re - im * h_im, re * h_im + im * h_re
        re, im = columns(re, im, INVERSE)
        re, im = lines(re, im, INVERSE)
        wave[0] = re
        wave[1] = im

        if step > 0:
            take_bottom(step, 1)
        wait_recv(step, FD, 1)
        gather(1)
        w_re, w_im = wave[0], wave[1]
        o_re, o_im = win[1, 0], win[1, 1]
        re, im = w_re * o_re - w_im * o_im, w_re * o_im + w_im * o_re
        re, im = lines(re, im, FORWARD)
        re, im = columns(re, im, FORWARD)
        seen = jnp.concatenate([measured[k] for k in range(SLOTS)], axis=1)
        slot = lax.broadcasted_iota(jnp.int32, (N, SLOTS * N), 1) // N
        factor = 2.0 * (re * re + im * im - seen)
        factor = jnp.where(slot < counts[0, 0], factor, 0.0)
        re, im = columns(re * factor, im * factor, INVERSE)
        re, im = lines(re, im, INVERSE)
        scatter(w_re * re + w_im * im, w_re * im - w_im * re)
        wave[0] = o_re * re + o_im * im
        wave[1] = o_re * im - o_im * re

        send_back(step, 1)
        re, im = lines(wave[0], wave[1], FORWARD)
        re, im = columns(re, im, FORWARD)
        re, im = h_re * re + h_im * im, h_re * im - h_im * re
        re, im = columns(re, im, INVERSE)
        re, im = lines(re, im, INVERSE)
        send_side(step, 1)
        scatter(p_re * re + p_im * im, p_re * im - p_im * re)
        send_back(step, 0)
        send_partly(step, 1)
        send_side(step, 0)
        send_partly(step, 0)
        finish(step, 1)
        finish(step, 0)

    wait_send(0, FR, 1)
    wait_send(0, FB, 1)
    for step in range(ITERS):
        for s in range(2):

            @pl.when(corner_down)
            def _():
                wait_send(step, GD, s)

            @pl.when(corner_right)
            def _():
                wait_send(step, GE, s)

            wait_send(step, GB, s)
            wait_send(step, GR, s)
            if step > 0:
                wait_send(step, FR, s)
                wait_send(step, FB, s)

                @pl.when(passes_up)
                def _():
                    wait_send(step, FD, s)

                @pl.when(passes_left)
                def _():
                    wait_send(step, FE, s)


def per_device(object_slices, probe, phase, positions, counts, measured):
    rights, lefts = dft_tables()
    vmem = pl.BlockSpec(memory_space=pltpu.VMEM)
    hbm = pl.BlockSpec(memory_space=pltpu.HBM)
    f32 = jnp.float32
    return pl.pallas_call(
        functools.partial(kernel, (lax.axis_size("row"), lax.axis_size("col"))),
        out_shape=jax.ShapeDtypeStruct((2, 2, N, N), f32),
        in_specs=[hbm, pl.BlockSpec(memory_space=pl.ANY)] + [hbm] * 6,
        out_specs=vmem,
        scratch_shapes=[
            pltpu.VMEM((2, 2, 2 * N, N), f32),
            pltpu.VMEM((2, 2, 2 * N, N), f32),
            pltpu.VMEM((2, 2, N, SLOTS * N), f32),
            pltpu.VMEM((2, N, SLOTS * N), f32),
            pltpu.VMEM((ITERS, 2, 4, 2, N, N), f32),
            pltpu.VMEM((ITERS, 2, 2, N, N), f32),
            pltpu.VMEM((ITERS, 2, 2, N, N), f32),
            pltpu.VMEM((ITERS, 2, 2, N, N), f32),
            pltpu.VMEM((ITERS, 2, 2, N, N), f32),
            pltpu.VMEM((2, 2, N, N), f32),
            pltpu.VMEM((2, 2, N, N), f32),
            pltpu.VMEM((SLOTS, 2, 2, 3 * N, N), f32),
            pltpu.SMEM((1, 1, 2, SLOTS), jnp.int32),
            pltpu.SMEM((1, 1), jnp.int32),
            pltpu.VMEM((2, N, N), f32),
            pltpu.VMEM((N, N), f32),
            pltpu.VMEM((SLOTS, N, N), f32),
            pltpu.VMEM((2, 6 * N, 2 * N), jnp.bfloat16),
            pltpu.VMEM((2, 2 * N, 6 * N), jnp.bfloat16),
            pltpu.VMEM((2, N, N), f32),
            pltpu.SemaphoreType.DMA((ITERS, 8, 2, 2)),
            pltpu.SemaphoreType.DMA((ITERS, 8, 2, 2)),
            pltpu.SemaphoreType.DMA((9,)),
        ],
        compiler_params=pltpu.CompilerParams(
            collective_id=0, has_side_effects=True, vmem_limit_bytes=56 * 1024 * 1024
        ),
        cost_estimate=pl.CostEstimate(
            flops=6 * 805306368, bytes_accessed=2500000, transcendentals=0
        ),
    )(
        positions.transpose(0, 1, 3, 2),
        counts,
        object_slices,
        probe,
        phase,
        measured.reshape(SLOTS, N, N),
        jnp.asarray(rights),
        jnp.asarray(lefts),
    )


def solution(mesh):
    return jax.shard_map(
        per_device,
        mesh=mesh,
        in_specs=(
            P(None, None, "row", "col"),
            P(),
            P(),
            P("row", "col", None, None),
            P("row", "col"),
            P("row", "col", None, None, None),
        ),
        out_specs=P(None, None, "row", "col"),
        check_vma=False,
    )
```

time: 72 us -> 74.2 us (1.031)
  the two profiles are of different devices: /device:TPU:1 before, /device:TPU:2 now
where the time goes in v3:
time: 74.2 us; the launch traced here: 73.5 us
  Pallas kernels  71.1 us (96%)
  local copies, waits for them, and re-layouts  1.67 us (2%)
    pallas_call x1, Pallas kernels, per_device(): pl.pallas_call(functools.partial(kernel, (lax.axis_size('row'), lax.axis_...  71.1 us
    unnamed x1, local copies, waits for them, and re-layouts  1.67 us

profile of v3, /device:TPU:2, one launch (start us, length us, event | category | flops | bytes accessed | tf_op | source)
XLA Modules:
  0.0 73.5 jit_solution(7371759302824657361)
XLA Ops:
  0.7 71.1 %shard_map.82 = f32[2,2,128,128]{3,2,1,0:T(8,128)} custom-call(s32[1,1,2,4]{3,2,1,0:T(2,128)} %bitcast.3, s32[1,1]{1,0:T(1,128)S(6)} %copy.10.count_hbm, f32[2,2,128,128]{3,2,1,0:T(8,128)} %obj_hbm.1, f32[2,128,128]{2,1,0:T(8,128)} %probe_hbm.1, f32[128,128]{1,0:T(8,128)} %phase_hbm.1, f32[4,128,128]{2,1,0:T(8,128)} %bitcast.2, ...), custom_call_target="tpu_custom_call" | custom-call | flops 4831838208 | bytes 2500000 | tf_op jit(solution)/shard_map/pallas_call | solution.py:409
  71.8 1.7 %copy.11 = f32[2,2,128,128]{3,2,1,0:T(8,128)} copy(f32[2,2,128,128]{3,2,1,0:T(8,128)} %shard_map.82) | data formatting | bytes 524288

commit v4 on v3

--- a/solution.py
+++ b/solution.py
@@ -14,7 +14,7 @@
 N = 128
 SLOTS = 4
 
-FR, FB, FD, GD, GB, GR, FE, GE = range(8)
+FR, FB, FD, GD, GB, GR, FE, GE, FX, GX = range(10)
 RUN = 8
 FORWARD, INVERSE = 0, 1
 
@@ -80,11 +80,36 @@
     right = (row, lax.rem(col + 1, cols))
     above = (lax.rem(row + rows - 1, rows), col)
     below = (lax.rem(row + 1, rows), col)
+    above_left, below_right = (above[0], left[1]), (below[0], right[1])
     exts = (ext0, ext1)
+
+    row_end, row_start = lax.rem(row, RUN) == RUN - 1, lax.rem(row, RUN) == 0
+    col_end, col_start = lax.rem(col, RUN) == RUN - 1, lax.rem(col, RUN) == 0
+    col_edge = col_end | col_start
+    passes_up = jnp.logical_not(row_start & col_edge)
+    passes_left = row_end & (lax.rem(col, RUN) == 1)
+    sends_diagonal = row_start & col_start
+    corner_down = jnp.logical_not(row_end & col_edge)
+    corner_right = row_end & col_start
+    corner_diagonal = row_end & col_end
+    corner_from_above = passes_up
+    corner_from_left = passes_left
+    corner_from_diagonal = sends_diagonal
 
     barrier = pltpu.get_barrier_semaphore()
     for neighbour in (left, right, above, below):
         pl.semaphore_signal(barrier, inc=1, device_id=neighbour, device_id_type=MESH)
+    for takes_part, neighbour in (
+        (sends_diagonal, above_left),
+        (corner_diagonal, below_right),
+    ):
+
+        @pl.when(takes_part)
+        def _():
+            pl.semaphore_signal(
+                barrier, inc=1, device_id=neighbour, device_id_type=MESH
+            )
+
 
     def local(source, target, sem):
         return pltpu.make_async_copy(source, target, local_sem.at[sem])
@@ -102,15 +127,6 @@
     for copy in argument_copies:
         copy.start()
 
-    row_end, row_start = lax.rem(row, RUN) == RUN - 1, lax.rem(row, RUN) == 0
-    col_end, col_start = lax.rem(col, RUN) == RUN - 1, lax.rem(col, RUN) == 0
-    passes_up = jnp.logical_not(row_start & col_end)
-    passes_left = row_end & col_start
-    corner_down = jnp.logical_not(row_end & col_start)
-    corner_right = row_end & col_start
-    corner_from_above = jnp.logical_not(row_start & col_start)
-    corner_from_left = row_end & (lax.rem(col, RUN) == 1)
-
     def piece(step, kind, s, c):
         ext = exts[s]
         side, bottom = ext.at[1, c, 0:N, :], ext.at[0, c, N : 2 * N, :]
@@ -123,11 +139,13 @@
             FD: (side, corner, above),
             FE: (bottom, corner, left),
             GD: (grad.at[step, s, 3, c], in_corner.at[step, s, c], below),
+            FX: (own if step else obj_hbm.at[s, c], corner, above_left),
+            GX: (grad.at[step, s, 3, c], in_extra.at[step, s, c], below_right),
             GE: (grad.at[step, s, 3, c], in_extra.at[step, s, c], right),
             GB: (grad.at[step, s, 2, c], in_bottom.at[step, s, c], below),
             GR: (grad.at[step, s, 1, c], in_side.at[step, s, c], right),
         }[kind]
-        landing = FD if kind == FE else kind
+        landing = {FE: FD, FX: FD, GX: GE}.get(kind, kind)
         return pltpu.make_async_remote_copy(
             src_ref=source,
             dst_ref=target,
@@ -208,9 +226,16 @@
             scatter_slot(k, 0, re[:, k * N : (k + 1) * N])
             scatter_slot(k, 1, im[:, k * N : (k + 1) * N])
 
-    pl.semaphore_wait(barrier, 4)
+    pl.semaphore_wait(barrier, jnp.where(sends_diagonal | corner_diagonal, 5, 4))
+
+    def send_diagonal(step, s):
+        @pl.when(sends_diagonal)
+        def _():
+            start(step, FX, s)
+
     start(0, FR, 0)
     start(0, FB, 0)
+    send_diagonal(0, 0)
 
     for copy in argument_copies:
         copy.wait()
@@ -227,6 +252,7 @@
     start(0, FB, 1)
     wait_send(0, FR, 0)
     start(0, FR, 1)
+    send_diagonal(0, 1)
 
     def pass_side_up(step, s, c):
         @pl.when(passes_up)
@@ -266,6 +292,10 @@
         @pl.when(corner_right)
         def _():
             start(step, GE, s)
+
+        @pl.when(corner_diagonal)
+        def _():
+            start(step, GX, s)
 
         collect(step, s, 2)
 
@@ -295,6 +325,11 @@
 
     def send_partly(step, s):
         for c in range(2):
+            @pl.when(corner_from_diagonal)
+            def _():
+                piece(step, GX, s, c).wait_recv()
+                grad[step, s, 0, c] = grad[step, s, 0, c] + in_extra[step, s, c]
+
             piece(step, GB, s, c).wait_recv()
             total = grad[step, s, 0, c] + in_bottom[step, s, c]
             new = exts[s][0, c, 0:N, :] - STEP_RATE * total
@@ -313,6 +348,11 @@
                 new = partly[s, c] - STEP_RATE * in_side[step, s, c]
                 exts[s][0, c, 0:N, :] = new
                 piece(step + 1, FB, s, c).start()
+
+                @pl.when(sends_diagonal)
+                def _():
+                    piece(step + 1, FX, s, c).start()
+
                 piece(step + 1, FR, s, c).wait_recv()
                 exts[s][1, c, 0:N, :] = in_right[s, c] - STEP_RATE * grad[step, s, 1, c]
                 pass_side_up(step + 1, s, c)
@@ -385,6 +425,14 @@
             @pl.when(corner_right)
             def _():
                 wait_send(step, GE, s)
+
+            @pl.when(corner_diagonal)
+            def _():
+                wait_send(step, GX, s)
+
+            @pl.when(sends_diagonal)
+            def _():
+                wait_send(step, FX, s)
 
             wait_send(step, GB, s)
             wait_send(step, GR, s)
@@ -432,8 +480,8 @@
             pltpu.VMEM((2, 6 * N, 2 * N), jnp.bfloat16),
             pltpu.VMEM((2, 2 * N, 6 * N), jnp.bfloat16),
             pltpu.VMEM((2, N, N), f32),
-            pltpu.SemaphoreType.DMA((ITERS, 8, 2, 2)),
-            pltpu.SemaphoreType.DMA((ITERS, 8, 2, 2)),
+            pltpu.SemaphoreType.DMA((ITERS, 10, 2, 2)),
+            pltpu.SemaphoreType.DMA((ITERS, 10, 2, 2)),
             pltpu.SemaphoreType.DMA((9,)),
         ],
         compiler_params=pltpu.CompilerParams(

time: 74.2 us -> 65.3 us (0.88)
  the two profiles are of different devices: /device:TPU:2 before, /device:TPU:64 now
where the time goes in v4:
time: 65.3 us; the launch traced here: 65.1 us
  Pallas kernels  62.8 us (96%)
  local copies, waits for them, and re-layouts  1.67 us (3%)
  between operations  0.66 us (1%)
    pallas_call x1, Pallas kernels, per_device(): pl.pallas_call(functools.partial(kernel, (lax.axis_size('row'), lax.axis_...  62.8 us
    unnamed x1, local copies, waits for them, and re-layouts  1.67 us

profile of v4, /device:TPU:64, one launch (start us, length us, event | category | flops | bytes accessed | tf_op | source)
XLA Modules:
  0.0 65.1 jit_solution(2772934773365317212)
XLA Ops:
  0.7 62.8 %shard_map.82 = f32[2,2,128,128]{3,2,1,0:T(8,128)} custom-call(s32[1,1,2,4]{3,2,1,0:T(2,128)} %bitcast.3, s32[1,1]{1,0:T(1,128)S(6)} %copy.10.count_hbm, f32[2,2,128,128]{3,2,1,0:T(8,128)} %obj_hbm.1, f32[2,128,128]{2,1,0:T(8,128)} %probe_hbm.1, f32[128,128]{1,0:T(8,128)} %phase_hbm.1, f32[4,128,128]{2,1,0:T(8,128)} %bitcast.2, ...), custom_call_target="tpu_custom_call" | custom-call | flops 4831838208 | bytes 2500000 | tf_op jit(solution)/shard_map/pallas_call | solution.py:457
  63.5 1.7 %copy.11 = f32[2,2,128,128]{3,2,1,0:T(8,128)} copy(f32[2,2,128,128]{3,2,1,0:T(8,128)} %shard_map.82) | data formatting | bytes 524288

commit v5 on v4

--- a/solution.py
+++ b/solution.py
@@ -15,6 +15,7 @@
 SLOTS = 4
 
 FR, FB, FD, GD, GB, GR, FE, GE, FX, GX = range(10)
+DETOUR = (1,)
 RUN = 8
 FORWARD, INVERSE = 0, 1
 
@@ -85,16 +86,20 @@
 
     row_end, row_start = lax.rem(row, RUN) == RUN - 1, lax.rem(row, RUN) == 0
     col_end, col_start = lax.rem(col, RUN) == RUN - 1, lax.rem(col, RUN) == 0
-    col_edge = col_end | col_start
-    passes_up = jnp.logical_not(row_start & col_edge)
-    passes_left = row_end & (lax.rem(col, RUN) == 1)
+    next_col = lax.rem(col, RUN) == 1
     sends_diagonal = row_start & col_start
-    corner_down = jnp.logical_not(row_end & col_edge)
-    corner_right = row_end & col_start
     corner_diagonal = row_end & col_end
-    corner_from_above = passes_up
-    corner_from_left = passes_left
-    corner_from_diagonal = sends_diagonal
+
+    def turns(step, s):
+        return step > 0 and s in DETOUR
+
+    def passes_up(step, s):
+        return jnp.logical_not(
+            row_start & (col_end | col_start if turns(step, s) else col_end)
+        )
+
+    def corner_edge(s):
+        return col_end | col_start if s in DETOUR else col_end
 
     barrier = pltpu.get_barrier_semaphore()
     for neighbour in (left, right, above, below):
@@ -181,18 +186,20 @@
                 win[s, c, :, k * N : (k + 1) * N] = mixed
 
     def scatter_slot(k, c, value):
-        q = positions[0, 0, 1, k]
-        moved = pltpu.roll(value, q, 1)
-        pad[k, 0, c, N : 2 * N, :] = jnp.where(lane >= q, moved, 0.0)
-        pad[k, 1, c, N : 2 * N, :] = jnp.where(lane < q, moved, 0.0)
-
-    def collect(step, s, quadrant):
-        v, h = quadrant // 2, quadrant % 2
-        for c in range(2):
-            total = pad[0, h, c, pl.ds((v + 1) * N - positions[0, 0, 0, 0], N), :]
-            for k in range(1, SLOTS):
-                total += pad[k, h, c, pl.ds((v + 1) * N - positions[0, 0, 0, k], N), :]
-            grad[step, s, quadrant, c] = total
+        pad[k, c, N : 2 * N, :] = pltpu.roll(value, positions[0, 0, 1, k], 1)
+
+    def collect(step, s, v):
+        for c in range(2):
+            near = far = None
+            for k in range(SLOTS):
+                q = positions[0, 0, 1, k]
+                moved = pad[k, c, pl.ds((v + 1) * N - positions[0, 0, 0, k], N), :]
+                first = jnp.where(lane >= q, moved, 0.0)
+                second = jnp.where(lane < q, moved, 0.0)
+                near = first if near is None else near + first
+                far = second if far is None else far + second
+            grad[step, s, 2 * v, c] = near
+            grad[step, s, 2 * v + 1, c] = far
 
     def columns(re, im, which):
         high, low = split(jnp.concatenate([re, im], axis=0))
@@ -236,6 +243,9 @@
     start(0, FR, 0)
     start(0, FB, 0)
     send_diagonal(0, 0)
+    start(0, FR, 1)
+    start(0, FB, 1)
+    send_diagonal(0, 1)
 
     for copy in argument_copies:
         copy.wait()
@@ -243,29 +253,26 @@
     prop[1] = jnp.sin(phase_ref[...])
     zero = jnp.zeros((N, N), jnp.float32)
     for k in range(SLOTS):
-        for h in range(2):
-            for c in range(2):
-                pad[k, h, c, 0:N, :] = zero
-                pad[k, h, c, 2 * N : 3 * N, :] = zero
+        for c in range(2):
+            pad[k, c, 0:N, :] = zero
+            pad[k, c, 2 * N : 3 * N, :] = zero
 
     wait_send(0, FB, 0)
-    start(0, FB, 1)
     wait_send(0, FR, 0)
-    start(0, FR, 1)
-    send_diagonal(0, 1)
 
     def pass_side_up(step, s, c):
-        @pl.when(passes_up)
+        @pl.when(passes_up(step, s))
         def _():
             piece(step, FD, s, c).start()
 
     def take_bottom(step, s):
         for c in range(2):
             piece(step, FB, s, c).wait_recv()
-
-            @pl.when(passes_left)
-            def _():
-                piece(step, FE, s, c).start()
+            if turns(step, s):
+
+                @pl.when(row_end & next_col)
+                def _():
+                    piece(step, FE, s, c).start()
 
     def first_halo(s):
         for c in range(2):
@@ -275,48 +282,50 @@
 
     def send_back(step, s):
         if step == 0:
-            @pl.when(passes_up)
+            @pl.when(passes_up(0, s))
             def _():
                 wait_send(0, FD, s)
 
-            @pl.when(passes_left)
-            def _():
-                wait_send(0, FE, s)
-
-        collect(step, s, 3)
-
-        @pl.when(corner_down)
+        collect(step, s, 1)
+
+        @pl.when(jnp.logical_not(row_end & corner_edge(s)))
         def _():
             start(step, GD, s)
-
-        @pl.when(corner_right)
-        def _():
-            start(step, GE, s)
 
         @pl.when(corner_diagonal)
         def _():
             start(step, GX, s)
 
-        collect(step, s, 2)
-
-        @pl.when(jnp.logical_not(corner_from_left))
-        def _():
+        if s in DETOUR:
+
+            @pl.when(row_end & col_start)
+            def _():
+                start(step, GE, s)
+
+        if s in DETOUR:
+
+            @pl.when(jnp.logical_not(row_end & next_col))
+            def _():
+                start(step, GB, s)
+
+        else:
             start(step, GB, s)
-
-        collect(step, s, 1)
         collect(step, s, 0)
 
-        @pl.when(corner_from_left)
-        def _():
-            for c in range(2):
-                piece(step, GE, s, c).wait_recv()
-                grad[step, s, 2, c] = grad[step, s, 2, c] + in_extra[step, s, c]
-                piece(step, GB, s, c).start()
+    def send_turned(step, s):
+        if s in DETOUR:
+
+            @pl.when(row_end & next_col)
+            def _():
+                for c in range(2):
+                    piece(step, GE, s, c).wait_recv()
+                    grad[step, s, 2, c] = grad[step, s, 2, c] + in_extra[step, s, c]
+                    piece(step, GB, s, c).start()
 
     def send_side(step, s):
         for c in range(2):
 
-            @pl.when(corner_from_above)
+            @pl.when(jnp.logical_not(row_start & corner_edge(s)))
             def _():
                 piece(step, GD, s, c).wait_recv()
                 grad[step, s, 1, c] = grad[step, s, 1, c] + in_corner[step, s, c]
@@ -325,7 +334,7 @@
 
     def send_partly(step, s):
         for c in range(2):
-            @pl.when(corner_from_diagonal)
+            @pl.when(sends_diagonal)
             def _():
                 piece(step, GX, s, c).wait_recv()
                 grad[step, s, 0, c] = grad[step, s, 0, c] + in_extra[step, s, c]
@@ -364,8 +373,8 @@
             take_bottom(step, 0)
         wait_recv(step, FD, 0)
         gather(0)
-        if step == 0:
-            first_halo(1)
+        if step > 0:
+            take_bottom(step, 1)
 
         p_re, p_im = for_all(probe_ref[0]), for_all(probe_ref[1])
         h_re, h_im = for_all(prop[0]), for_all(prop[1])
@@ -373,14 +382,14 @@
         re, im = p_re * o_re - p_im * o_im, p_re * o_im + p_im * o_re
         re, im = lines(re, im, FORWARD)
         re, im = columns(re, im, FORWARD)
+        if step == 0:
+            first_halo(1)
         re, im = re * h_re - im * h_im, re * h_im + im * h_re
         re, im = columns(re, im, INVERSE)
         re, im = lines(re, im, INVERSE)
         wave[0] = re
         wave[1] = im
 
-        if step > 0:
-            take_bottom(step, 1)
         wait_recv(step, FD, 1)
         gather(1)
         w_re, w_im = wave[0], wave[1]
@@ -405,10 +414,26 @@
         re, im = columns(re, im, INVERSE)
         re, im = lines(re, im, INVERSE)
         send_side(step, 1)
+        send_turned(step, 1)
         scatter(p_re * re + p_im * im, p_re * im - p_im * re)
         send_back(step, 0)
-        send_partly(step, 1)
-        send_side(step, 0)
+        if 1 in DETOUR:
+            late = row_start & next_col
+
+            @pl.when(late)
+            def _():
+                send_side(step, 0)
+                send_partly(step, 1)
+
+            @pl.when(jnp.logical_not(late))
+            def _():
+                send_partly(step, 1)
+                send_side(step, 0)
+
+        else:
+            send_partly(step, 1)
+            send_side(step, 0)
+        send_turned(step, 0)
         send_partly(step, 0)
         finish(step, 1)
         finish(step, 0)
@@ -418,13 +443,15 @@
     for step in range(ITERS):
         for s in range(2):
 
-            @pl.when(corner_down)
+            @pl.when(jnp.logical_not(row_end & corner_edge(s)))
             def _():
                 wait_send(step, GD, s)
 
-            @pl.when(corner_right)
-            def _():
-                wait_send(step, GE, s)
+            if s in DETOUR:
+
+                @pl.when(row_end & col_start)
+                def _():
+                    wait_send(step, GE, s)
 
             @pl.when(corner_diagonal)
             def _():
@@ -440,13 +467,15 @@
                 wait_send(step, FR, s)
                 wait_send(step, FB, s)
 
-                @pl.when(passes_up)
+                @pl.when(passes_up(step, s))
                 def _():
                     wait_send(step, FD, s)
 
-                @pl.when(passes_left)
-                def _():
-                    wait_send(step, FE, s)
+                if turns(step, s):
+
+                    @pl.when(row_end & next_col)
+                    def _():
+                        wait_send(step, FE, s)
 
 
 def per_device(object_slices, probe, phase, positions, counts, measured):
@@ -471,7 +500,7 @@
             pltpu.VMEM((ITERS, 2, 2, N, N), f32),
             pltpu.VMEM((2, 2, N, N), f32),
             pltpu.VMEM((2, 2, N, N), f32),
-            pltpu.VMEM((SLOTS, 2, 2, 3 * N, N), f32),
+            pltpu.VMEM((SLOTS, 2, 3 * N, N), f32),
             pltpu.SMEM((1, 1, 2, SLOTS), jnp.int32),
             pltpu.SMEM((1, 1), jnp.int32),
             pltpu.VMEM((2, N, N), f32),

time: 65.3 us -> 64.1 us (0.982)
  the two profiles are of different devices: /device:TPU:64 before, /device:TPU:2 now
where the time goes in v5:
time: 64.1 us; the launch traced here: 64 us
  Pallas kernels  61.6 us (96%)
  local copies, waits for them, and re-layouts  1.67 us (3%)
  between operations  0.66 us (1%)
    pallas_call x1, Pallas kernels, per_device(): pl.pallas_call(functools.partial(kernel, (lax.axis_size('row'), lax.axis_...  61.6 us
    unnamed x1, local copies, waits for them, and re-layouts  1.67 us

profile of v5, /device:TPU:2, one launch (start us, length us, event | category | flops | bytes accessed | tf_op | source)
XLA Modules:
  0.0 64.0 jit_solution(10383496189245622712)
XLA Ops:
  0.7 61.6 %shard_map.82 = f32[2,2,128,128]{3,2,1,0:T(8,128)} custom-call(s32[1,1,2,4]{3,2,1,0:T(2,128)} %bitcast.3, s32[1,1]{1,0:T(1,128)S(6)} %copy.10.count_hbm, f32[2,2,128,128]{3,2,1,0:T(8,128)} %obj_hbm.1, f32[2,128,128]{2,1,0:T(8,128)} %probe_hbm.1, f32[128,128]{1,0:T(8,128)} %phase_hbm.1, f32[4,128,128]{2,1,0:T(8,128)} %bitcast.2, ...), custom_call_target="tpu_custom_call" | custom-call | flops 4831838208 | bytes 2500000 | tf_op jit(solution)/shard_map/pallas_call | solution.py:486
  62.3 1.7 %copy.11 = f32[2,2,128,128]{3,2,1,0:T(8,128)} copy(f32[2,2,128,128]{3,2,1,0:T(8,128)} %shard_map.82) | data formatting | bytes 524288

commit v6 on v5

--- a/solution.py
+++ b/solution.py
@@ -15,7 +15,7 @@
 SLOTS = 4
 
 FR, FB, FD, GD, GB, GR, FE, GE, FX, GX = range(10)
-DETOUR = (1,)
+DETOUR = (0, 1)
 RUN = 8
 FORWARD, INVERSE = 0, 1
 

time: 64.1 us -> 63.3 us (0.988); the launches traced: 64 us -> 62.3 us
  Pallas kernels: 61.6 us -> 59.9 us
    pallas_call x1, Pallas kernels: 61.6 us -> 59.9 us  [per_device(): pl.pallas_call(functools.partial(kernel, (lax.axis_size('row'), lax.axis_...]
where the time goes in v6:
time: 63.3 us; the launch traced here: 62.3 us
  Pallas kernels  59.9 us (95%)
  local copies, waits for them, and re-layouts  1.67 us (3%)
  between operations  0.66 us (1%)
    pallas_call x1, Pallas kernels, per_device(): pl.pallas_call(functools.partial(kernel, (lax.axis_size('row'), lax.axis_...  59.9 us
    unnamed x1, local copies, waits for them, and re-layouts  1.67 us

profile of v6, /device:TPU:2, one launch (start us, length us, event | category | flops | bytes accessed | tf_op | source)
XLA Modules:
  0.0 62.3 jit_solution(6595787969046269165)
XLA Ops:
  0.7 59.9 %shard_map.82 = f32[2,2,128,128]{3,2,1,0:T(8,128)} custom-call(s32[1,1,2,4]{3,2,1,0:T(2,128)} %bitcast.3, s32[1,1]{1,0:T(1,128)S(6)} %copy.10.count_hbm, f32[2,2,128,128]{3,2,1,0:T(8,128)} %obj_hbm.1, f32[2,128,128]{2,1,0:T(8,128)} %probe_hbm.1, f32[128,128]{1,0:T(8,128)} %phase_hbm.1, f32[4,128,128]{2,1,0:T(8,128)} %bitcast.2, ...), custom_call_target="tpu_custom_call" | custom-call | flops 4831838208 | bytes 2500000 | tf_op jit(solution)/shard_map/pallas_call | solution.py:486
  60.6 1.7 %copy.11 = f32[2,2,128,128]{3,2,1,0:T(8,128)} copy(f32[2,2,128,128]{3,2,1,0:T(8,128)} %shard_map.82) | data formatting | bytes 524288

commit v7 on v6

--- a/solution.py
+++ b/solution.py
@@ -382,10 +382,10 @@
         re, im = p_re * o_re - p_im * o_im, p_re * o_im + p_im * o_re
         re, im = lines(re, im, FORWARD)
         re, im = columns(re, im, FORWARD)
+        re, im = re * h_re - im * h_im, re * h_im + im * h_re
+        re, im = columns(re, im, INVERSE)
         if step == 0:
             first_halo(1)
-        re, im = re * h_re - im * h_im, re * h_im + im * h_re
-        re, im = columns(re, im, INVERSE)
         re, im = lines(re, im, INVERSE)
         wave[0] = re
         wave[1] = im
@@ -417,7 +417,11 @@
         send_turned(step, 1)
         scatter(p_re * re + p_im * im, p_re * im - p_im * re)
         send_back(step, 0)
-        if 1 in DETOUR:
+        if step == ITERS - 1:
+            send_side(step, 0)
+            send_turned(step, 0)
+            send_partly(step, 1)
+        elif 1 in DETOUR:
             late = row_start & next_col
 
             @pl.when(late)
@@ -433,7 +437,8 @@
         else:
             send_partly(step, 1)
             send_side(step, 0)
-        send_turned(step, 0)
+        if step < ITERS - 1:
+            send_turned(step, 0)
         send_partly(step, 0)
         finish(step, 1)
         finish(step, 0)

time: 63.3 us -> 63.2 us (level)
  no operation moved by 1% of the time
where the time goes in v7:
time: 63.2 us; the launch traced here: 62.3 us
  Pallas kernels  60 us (95%)
  local copies, waits for them, and re-layouts  1.67 us (3%)
  between operations  0.66 us (1%)
    pallas_call x1, Pallas kernels, per_device(): pl.pallas_call(functools.partial(kernel, (lax.axis_size('row'), lax.axis_...  60 us
    unnamed x1, local copies, waits for them, and re-layouts  1.67 us

profile of v7, /device:TPU:2, one launch (start us, length us, event | category | flops | bytes accessed | tf_op | source)
XLA Modules:
  0.0 62.3 jit_solution(3908321642073694909)
XLA Ops:
  0.7 60.0 %shard_map.82 = f32[2,2,128,128]{3,2,1,0:T(8,128)} custom-call(s32[1,1,2,4]{3,2,1,0:T(2,128)} %bitcast.3, s32[1,1]{1,0:T(1,128)S(6)} %copy.10.count_hbm, f32[2,2,128,128]{3,2,1,0:T(8,128)} %obj_hbm.1, f32[2,128,128]{2,1,0:T(8,128)} %probe_hbm.1, f32[128,128]{1,0:T(8,128)} %phase_hbm.1, f32[4,128,128]{2,1,0:T(8,128)} %bitcast.2, ...), custom_call_target="tpu_custom_call" | custom-call | flops 4831838208 | bytes 2500000 | tf_op jit(solution)/shard_map/pallas_call | solution.py:491
  60.6 1.7 %copy.11 = f32[2,2,128,128]{3,2,1,0:T(8,128)} copy(f32[2,2,128,128]{3,2,1,0:T(8,128)} %shard_map.82) | data formatting | bytes 524288
